TPU v7x, 32 devices: a whole 2x2x4 slice. The times are simulated.
32 devices in a mesh: experts: 4 (over z), context: 4 (over y, x), dp: 2 (over core).
Axes of the slice: x: 2, y: 2, z: 4, core: 2. Of those that a mesh axis runs over, the one named last changes fastest.
Arguments:
- tokens: bfloat16 [8, 1024, 768], P(('experts', 'dp'), 'context'), may hold values from -6 to 6
- cotangent: bfloat16 [8, 1024, 768], P(('experts', 'dp'), 'context'), may hold values from -6 to 6
- w_query: bfloat16 [768, 768], replicated, may hold values from -0.0546875 to 0.0546875
- w_key: bfloat16 [768, 768], replicated, may hold values from -0.21875 to 0.21875
- w_value: bfloat16 [768, 768], replicated, may hold values from -0.21875 to 0.21875
- w_output: bfloat16 [768, 768], replicated, may hold values from -1.75 to 1.75
- gain_attn: float32 [768], replicated, may hold values from 0.5 to 1.5
- gain_ffn: float32 [768], replicated, may hold values from 0.5 to 1.5
- bias_table: float32 [32, 12], replicated, may hold values from -4 to 4
- w_router: float32 [768, 8], replicated, may hold values from -0.15625 to 0.15625
- w_in: bfloat16 [8, 768, 3072], P('experts'), may hold values from -0.21875 to 0.21875
- w_out: bfloat16 [8, 3072, 768], P('experts'), may hold values from -3 to 3
- routes: int32 [8, 1024], P(('experts', 'dp'), 'context'), may hold values from 0 to 7
- slots: int32 [8, 1024], P(('experts', 'dp'), 'context'), may hold values from 0 to 95, as said below
- buckets: int32 [2047], replicated, may hold values from 0 to 31, as said below
Outputs:
- output: bfloat16 [8, 1024, 768], P(('experts', 'dp'), 'context')
- grad_tokens: float32 [8, 1024, 768], P(('experts', 'dp'), 'context')
- grad_query: float32 [768, 768], replicated
- grad_key: float32 [768, 768], replicated
- grad_value: float32 [768, 768], replicated
- grad_output: float32 [768, 768], replicated
- grad_gain_attn: float32 [768], replicated
- grad_gain_ffn: float32 [768], replicated
- grad_table: float32 [32, 12], replicated
- grad_router: float32 [768, 8], replicated
- grad_w_in: float32 [8, 768, 3072], P('experts', None, ('context', 'dp'))
- grad_w_out: float32 [8, 3072, 768], P('experts', ('context', 'dp'))
Inputs may be any that keep to these rules, and one draw needn't show every extreme that they name: Within one device's 256 tokens (aligned blocks of one sequence), the tokens routed to one expert hold distinct slots; a token whose slot is 64 or more is dropped from its expert. `buckets`: entry r + 1023 holds the bucket of the offset r = key position minus query position: under 32 // 2 for r <= 0 and 16 or more for r > 0; it does not fall as |r| grows on each side.
All inputs are finite; a program needn't handle non-finite values.
Results may differ from a plain program's by a relative error of at most 0.015.
The roundings to bfloat16 on the way count: a program that leaves them out, or rounds other values in their place, can miss the bound.
Values may be sent and summed in bfloat16 or wider, within the bound.
A program may use at most 192 MiB of HBM per device.

v0:
```python
import jax
import jax.numpy as jnp
from jax import lax
from jax.sharding import PartitionSpec as P


def rms_scale(value_rows, gain):
    return (
        value_rows
        * lax.rsqrt(jnp.mean(value_rows * value_rows, axis=-1, keepdims=True) + 1e-06)
        * gain
    )


def expert_slots(route_row, slot_row, expert_dev, n_owner, capacity, tok_count):
    kept = slot_row < capacity
    layout = (
        route_row % expert_dev * (n_owner * capacity)
        + route_row // expert_dev * capacity
        + slot_row
    )
    target = jnp.where(kept, layout, expert_dev * n_owner * capacity)
    empty_table = jnp.full((expert_dev * n_owner * capacity + 1,), tok_count, jnp.int32)
    slot_token = empty_table.at[target].set(jnp.arange(tok_count, dtype=jnp.int32))[:-1]
    read_index = jnp.where(kept, layout, 0)
    return (kept, slot_token, read_index)


def on_device(
    tokens,
    cotangent,
    w_query,
    w_key,
    w_value,
    w_output,
    gain_attn,
    gain_ffn,
    bias_table,
    w_router,
    w_in,
    w_out,
    routes,
    slots,
    buckets,
):
    tok_count = tokens.shape[1]
    width = tokens.shape[2]
    heads = bias_table.shape[1]
    bucket_count = bias_table.shape[0]
    head_dim = width // heads
    seq_len = tok_count * lax.axis_size("context")
    n_owner = lax.axis_size("experts")
    expert_dev = w_in.shape[0]
    capacity = 2 * tok_count // (expert_dev * n_owner)
    highest = lax.Precision.HIGHEST
    bfloat = jnp.bfloat16
    single = jnp.float32
    resid = tokens[0].astype(single)
    first_norm_output = rms_scale(resid, gain_attn).astype(bfloat)
    query_bf = jnp.dot(first_norm_output, w_query, preferred_element_type=single).astype(bfloat)
    key_halfwidth = jnp.dot(first_norm_output, w_key, preferred_element_type=single).astype(bfloat)
    value_bf = jnp.dot(first_norm_output, w_value, preferred_element_type=single).astype(bfloat)
    key_all, value_all = (
        lax.all_gather(key_halfwidth, "context", axis=0, tiled=True),
        lax.all_gather(value_bf, "context", axis=0, tiled=True),
    )
    query_pos = lax.axis_index("context") * tok_count + jnp.arange(tok_count, dtype=jnp.int32)
    offsets = jnp.arange(seq_len, dtype=jnp.int32)[None, :] - query_pos[:, None] + seq_len - 1
    bucket_map = buckets[offsets]
    position_hot = (
        bucket_map[:, :, None] == jnp.arange(bucket_count, dtype=jnp.int32)[None, None, :]
    ).astype(single)
    bias = jnp.einsum("qkb,bh->hqk", position_hot, bias_table, precision=highest)
    query_h = query_bf.reshape(tok_count, heads, head_dim)
    key_h = key_all.reshape(seq_len, heads, head_dim)
    value_h = value_all.reshape(seq_len, heads, head_dim)
    scores = jnp.einsum("qhd,khd->hqk", query_h, key_h, preferred_element_type=single) + bias
    top_score = jnp.max(scores, axis=-1, keepdims=True)
    log_total = top_score + jnp.log(jnp.sum(jnp.exp(scores - top_score), axis=-1, keepdims=True))
    probs_bf = jnp.exp(scores - log_total).astype(bfloat)
    attention_result = (
        jnp.einsum("hqk,khd->qhd", probs_bf, value_h, preferred_element_type=single)
        .reshape(tok_count, width)
        .astype(bfloat)
    )
    residual_middle = resid + jnp.dot(attention_result, w_output, preferred_element_type=single)
    norm_two = rms_scale(residual_middle, gain_ffn)
    logits = jnp.dot(norm_two, w_router, precision=highest)
    route_probs = jax.nn.softmax(logits, axis=-1)
    route_row = routes[0]
    route_hot = (
        route_row[:, None] == jnp.arange(logits.shape[1], dtype=jnp.int32)[None, :]
    ).astype(single)
    gate = jnp.sum(route_probs * route_hot, axis=-1)
    kept, slot_token, read_index = expert_slots(
        route_row, slots[0], expert_dev, n_owner, capacity, tok_count
    )
    zero_row = jnp.zeros((1, width), bfloat)
    send_rows = jnp.concatenate([norm_two.astype(bfloat), zero_row], axis=0)[slot_token]
    send_rows = send_rows.reshape(expert_dev, n_owner, capacity, width)
    arrived = lax.all_to_all(send_rows, "experts", split_axis=1, concat_axis=1, tiled=True).reshape(
        expert_dev, n_owner * capacity, width
    )
    pre_act = jnp.einsum("erd,edf->erf", arrived, w_in, preferred_element_type=single)
    act_bf = jax.nn.gelu(pre_act).astype(bfloat)
    expert_back = jnp.einsum("erf,efd->erd", act_bf, w_out, preferred_element_type=single).astype(
        bfloat
    )
    expert_back = expert_back.reshape(expert_dev, n_owner, capacity, width)
    returned = lax.all_to_all(
        expert_back, "experts", split_axis=1, concat_axis=1, tiled=True
    ).reshape(-1, width)
    routed = jnp.where(kept[:, None], returned[read_index].astype(single), 0.0)
    output = residual_middle + gate[:, None] * routed
    grad_out = cotangent[0].astype(single)
    grad_gate = jnp.sum(grad_out * routed, axis=-1)
    grad_routed = (grad_out * gate[:, None]).astype(bfloat)
    send_grads = jnp.concatenate([grad_routed, zero_row], axis=0)[slot_token]
    send_grads = send_grads.reshape(expert_dev, n_owner, capacity, width)
    grad_expert = lax.all_to_all(
        send_grads, "experts", split_axis=1, concat_axis=1, tiled=True
    ).reshape(expert_dev, n_owner * capacity, width)
    grad_act = jnp.einsum("erd,efd->erf", grad_expert, w_out, preferred_element_type=single)
    grad_pre = jax.vjp(jax.nn.gelu, pre_act)[1](grad_act)[0].astype(bfloat)
    grad_rows = jnp.einsum("erf,edf->erd", grad_pre, w_in, preferred_element_type=single).astype(
        bfloat
    )
    grad_rows = grad_rows.reshape(expert_dev, n_owner, capacity, width)
    whole_in = jnp.einsum("erd,erf->edf", arrived, grad_pre, preferred_element_type=single)
    whole_out = jnp.einsum("erf,erd->efd", act_bf, grad_expert, preferred_element_type=single)
    grad_w_in, grad_w_out = (
        lax.psum_scatter(
            whole_in.astype(jnp.bfloat16), ("context", "dp"), scatter_dimension=2, tiled=True
        ).astype(jnp.float32),
        lax.psum_scatter(
            whole_out.astype(jnp.bfloat16), ("context", "dp"), scatter_dimension=1, tiled=True
        ).astype(jnp.float32),
    )
    back_rows = lax.all_to_all(
        grad_rows, "experts", split_axis=1, concat_axis=1, tiled=True
    ).reshape(-1, width)
    grad_logits = grad_gate[:, None] * route_probs * (route_hot - gate[:, None])
    grad_router = jnp.einsum("td,te->de", norm_two, grad_logits, precision=highest)
    grad_norm_two = jnp.where(kept[:, None], back_rows[read_index].astype(single), 0.0)
    grad_norm_two = grad_norm_two + jnp.einsum(
        "te,de->td", grad_logits, w_router, precision=highest
    )
    grad_mid, grad_gain_ffn = jax.vjp(rms_scale, residual_middle, gain_ffn)[1](grad_norm_two)
    grad_mid = grad_mid + grad_out
    grad_attn = grad_mid.astype(bfloat)
    grad_output = jnp.einsum(
        "td,te->de", attention_result, grad_attn, preferred_element_type=single
    )
    grad_attended = jnp.einsum(
        "te,de->td", grad_attn, w_output, preferred_element_type=single
    ).astype(bfloat)
    grad_attended = grad_attended.reshape(tok_count, heads, head_dim)
    scores_again = jnp.einsum("qhd,khd->hqk", query_h, key_h, preferred_element_type=single) + bias
    probs_again = jnp.exp(scores_again - log_total)
    grad_probs = jnp.einsum("qhd,khd->hqk", grad_attended, value_h, preferred_element_type=single)
    inner_sum = jnp.sum(probs_again * grad_probs, axis=-1, keepdims=True)
    grad_scores = (probs_again * (grad_probs - inner_sum)).astype(bfloat)
    grad_q = (
        jnp.einsum("hqk,khd->qhd", grad_scores, key_h, preferred_element_type=single)
        .reshape(tok_count, width)
        .astype(bfloat)
    )
    key_part = jnp.einsum(
        "hqk,qhd->khd", grad_scores, query_h, preferred_element_type=single
    ).reshape(seq_len, width)
    value_part = jnp.einsum(
        "hqk,qhd->khd", probs_again.astype(bfloat), grad_attended, preferred_element_type=single
    ).reshape(seq_len, width)
    grad_table = jnp.einsum(
        "hqk,qkb->bh", grad_scores, position_hot.astype(bfloat), preferred_element_type=single
    )
    grad_k, grad_v = (
        lax.psum_scatter(
            key_part.astype(jnp.bfloat16), "context", scatter_dimension=0, tiled=True
        ).astype(jnp.float32),
        lax.psum_scatter(
            value_part.astype(jnp.bfloat16), "context", scatter_dimension=0, tiled=True
        ).astype(jnp.float32),
    )
    grad_k = grad_k.astype(bfloat)
    grad_v = grad_v.astype(bfloat)
    grad_query = jnp.einsum("td,te->de", first_norm_output, grad_q, preferred_element_type=single)
    grad_key = jnp.einsum("td,te->de", first_norm_output, grad_k, preferred_element_type=single)
    grad_value = jnp.einsum("td,te->de", first_norm_output, grad_v, preferred_element_type=single)
    grad_norm_one = jnp.einsum("te,de->td", grad_q, w_query, preferred_element_type=single)
    grad_norm_one = grad_norm_one + jnp.einsum(
        "te,de->td", grad_k, w_key, preferred_element_type=single
    )
    grad_norm_one = grad_norm_one + jnp.einsum(
        "te,de->td", grad_v, w_value, preferred_element_type=single
    )
    grad_resid, grad_gain_attn = jax.vjp(rms_scale, resid, gain_attn)[1](grad_norm_one)
    grad_tokens = grad_resid + grad_mid
    summed = lax.psum(
        (
            grad_query,
            grad_key,
            grad_value,
            grad_output,
            grad_gain_attn,
            grad_gain_ffn,
            grad_table,
            grad_router,
        ),
        ("experts", "context", "dp"),
    )
    return (
        output.astype(bfloat)[None],
        grad_tokens[None],
        summed[0],
        summed[1],
        summed[2],
        summed[3],
        summed[4],
        summed[5],
        summed[6],
        summed[7],
        grad_w_in,
        grad_w_out,
    )


def solution(mesh):
    in_specs = (
        P(("experts", "dp"), "context", None),
        P(("experts", "dp"), "context", None),
        P(),
        P(),
        P(),
        P(),
        P(),
        P(),
        P(),
        P(),
        P("experts", None, None),
        P("experts", None, None),
        P(("experts", "dp"), "context"),
        P(("experts", "dp"), "context"),
        P(),
    )
    out_specs = (
        P(("experts", "dp"), "context", None),
        P(("experts", "dp"), "context", None),
        P(),
        P(),
        P(),
        P(),
        P(),
        P(),
        P(),
        P(),
        P("experts", None, ("context", "dp")),
        P("experts", ("context", "dp"), None),
    )
    return jax.shard_map(
        on_device, mesh=mesh, in_specs=in_specs, out_specs=out_specs, check_vma=False
    )
```

profile of v0, /device:TPU:25, one launch (start us, length us, event | category | flops | bytes accessed | tf_op | source)
XLA Modules:
  0.0 3221.8 jit_solution(12708975468673859820)
XLA Ops:
  9.0 2.7 convolution_convert_fusion.8
  11.8 2.3 convolution_convert_fusion.10
  14.1 2.7 convolution_convert_fusion.9
  17.4 2561.6 %gather_fusion = s32[262144]{0:T(1024)} fusion(s32[2047]{0:T(1024)S(1)} %copy-done.1, s32[262144]{0:T(1024)S(1)} %broadcast_clamp_fusion), kind=kCustom, calls=%fused_computation | custom fusion | bytes 3145728 | tf_op jit(solution)/shard_map/gather | solution.py:69
  2580.8 12.8 fusion
  2594.4 15.8 copy.54
  2610.3 1.9 scatter_custom_fusion
  2614.0 7.1 fusion.78
  2621.1 2.6 exponential_reduce_fusion
  2628.0 7.3 fusion.15
  2636.2 2.7 gather_fusion.1
  2640.1 22.2 all_to_all.20
  2662.4 5.5 fusion.80
  2669.0 3.0 convolution_convert_fusion.5
  2672.9 5.6 all-to-all-start.1
  2681.3 13.4 all-to-all-done.1
  2697.3 2.1 fusion.35
  2699.4 2.8 gather_fusion.3
  2703.5 24.0 all_to_all.21
  2727.6 9.0 fusion.11
  2736.6 2.7 convolution_convert_fusion.4
  2739.4 22.5 all_to_all.22
  2762.0 2.1 gather_fusion.4
  2764.1 2.8 multiply_reduce_fusion.1
  2767.4 2.1 convert_add_fusion
  2769.6 2.8 convolution_convert_fusion.7
  2773.6 7.8 convolution_convert_fusion.2
  2781.5 7.1 multiply_reduce_fusion
  2788.6 6.6 multiply_convert_fusion
  2795.2 2.8 convolution_convert_fusion.3
  2798.4 7.1 convolution_convert_fusion.1
  2805.5 24.0 copy.69
  2829.5 9.3 copy.72
  2839.9 10.2 convolution_convert_fusion
  2850.3 5.4 convolution_convert_fusion.6
  2856.4 2.1 fusion.41
  2860.3 3.2 fusion.70
  2863.6 3.1 fusion.72
  2868.0 12.3 copy.64
  2880.3 1.9 fusion.81
  2882.2 7.0 fusion.18
  2890.5 40.4 %all-reduce.2 = (f32[768]{0:T(1024)}, f32[768]{0:T(1024)}, f32[32,12]{0,1:T(8,128)}, f32[768,8]{0,1:T(8,128)}) all-reduce(f32[768]{0:T(1024)S(1)} %get-tuple-element.14, f32[768]{0:T(1024)S(1)} %copy-done.56, f32[32,12]{0,1:T(8,128)S(1)} %fusion.18, ...), channel_id=1, replica_groups=mesh['experts'=4,'context'=4,'dp'=2] {'experts','context','dp'}, use_global_device_ids=true, to_apply=%region_19.20 | all-reduce | flops 8064 | bytes 64512 | tf_op jit(solution)/shard_map/psum | solution.py:199
  2932.1 2.9 reshape.431
  2935.1 2.0 copy.70
  2938.6 70.2 %reduce-scatter.11.cloned.1.call-done = bf16[2,384,768]{2,1,0:T(8,128)(2,1)} async-done(((bf16[2,3072,768]{2,1,0:T(8,128)(2,1)}), bf16[2,384,768]{2,1,0:T(8,128)(2,1)}) %reduce-scatter.11.cloned.1.call-update) | async-done | bytes 1179664 | tf_op jit(solution)/shard_map/reduce_scatter | solution.py:135
  3008.8 2.8 convert_element_type.177
  3011.6 195.2 %all-reduce.6.cloned.1.call-done = (f32[768,768]{1,0:T(8,128)}, f32[768,768]{1,0:T(8,128)}, f32[768,768]{1,0:T(8,128)}, f32[768,768]{1,0:T(8,128)}) async-done(((f32[768,768]{1,0:T(8,128)}, f32[768,768]{1,0:T(8,128)}, f32[768,768]{1,0:T(8,128)}, f32[768,768]{1,0:T(8,128)}), (f32[768,768]{1,0:T(8,128)}, f32[768,768]{1,0:T(8,128)}, f32[768,768]{1,0:T(8,128)}, ...) | async-done | bytes 9437200 | tf_op jit(solution)/shard_map/psum | solution.py:199
  3206.8 3.4 copy.77
  (213 shorter events, 37.3 us)
Async XLA Ops:
  7.2 2605.1 %all-gather.5.cloned.1.call-start = ((), (), s32[]{:S(2)}) async-start(), calls=%async_computation.9 | async-start | bytes 1966080 | tf_op jit(solution)/shard_map/all_gather | solution.py:64
  9.0 8.2 copy-start.44
  9.0 8.4 copy-start.1
  11.7 2614.5 %all-gather.3.cloned.1.call-start = ((), (), s32[]{:S(2)}) async-start(), calls=%async_computation.8 | async-start | bytes 1966080 | tf_op jit(solution)/shard_map/all_gather | solution.py:65
  17.4 2563.4 %copy-start.62 = (f32[32,12]{0,1:T(8,128)S(1)}, f32[32,12]{0,1:T(8,128)}, u32[]{:S(2)}) copy-start(f32[32,12]{0,1:T(8,128)} %param.23) | copy-start | bytes 4612
  2580.8 12.9 copy-start.14
  2580.8 12.9 copy-start.53
  2580.8 12.9 copy-start.63
  2580.8 13.4 copy-start.32
  2594.4 19.6 copy-start.12
  2612.2 23.9 copy-start.57
  2614.0 7.1 copy-start.6
  2628.0 7.3 copy-start.7
  2628.0 7.3 copy-start.5
  2628.0 7.3 copy-start.16
  2628.0 7.9 copy-start.35
  2669.0 9.7 copy-start.65
  2669.0 10.3 copy-start.64
  2669.0 10.9 copy-start.38
  2669.0 10.9 copy-start.41
  2669.0 11.8 copy-start.54
  2672.9 21.8 all-to-all-start.1
  2678.5 181.8 %reduce-scatter.9.cloned.1.call-start = ((), (), s32[]{:S(2)}) async-start(), calls=%async_computation.11 | async-start | bytes 1966080 | tf_op jit(solution)/shard_map/reduce_scatter | solution.py:181
  2680.7 15.2 copy-start.47
  2680.8 18.7 copy-start.51
  2681.3 18.1 copy-start.49
  2703.5 33.1 %slice-start = ((s8[9437184]{0:T(1024)(128)(4,1)}), s8[4194304]{0:T(1024)(128)(4,1)S(1)}, s32[]{:S(2)}) async-start(s8[9437184]{0:T(1024)(128)(4,1)} %bitcast.159), calls=%async_computation.15 | async-start | bytes 8388608
  2727.5 9.1 copy-start.29
  2727.5 9.1 slice-start.1
  2727.5 9.1 slice-start.2
  2739.3 24.7 copy-start.34
  2739.3 24.7 copy-start.42
  2739.3 28.1 copy-start.19
  2769.6 11.8 copy-start.10
  2781.4 7.1 copy-start.31
  2781.4 82.1 %reduce-scatter.7.cloned.1.call-start = ((), (), s32[]{:S(2)}) async-start(), calls=%async_computation.10 | async-start | bytes 1966080 | tf_op jit(solution)/shard_map/reduce_scatter | solution.py:178
  2798.3 133.8 %reduce-scatter.13.cloned.1.call-start = ((), (), s32[]{:S(2)}) async-start(), calls=%async_computation.13 | async-start | bytes 10616832
  2838.8 170.0 %reduce-scatter.11.cloned.1.call-start = ((), (), s32[]{:S(2)}) async-start(), calls=%async_computation.12 | async-start | bytes 10616832 | tf_op jit(solution)/shard_map/reduce_scatter | solution.py:135
  2850.2 8.3 copy-start.11
  2850.2 8.3 copy-start.21
  2850.2 356.6 %all-reduce.6.cloned.1.call-start = ((), (), s32[]{:S(2)}) async-start(), calls=%async_computation.14 | async-start | bytes 18874368 | tf_op jit(solution)/shard_map/psum | solution.py:199
  2868.0 14.2 copy-start.15
  2882.2 7.0 copy-start.27
  2882.2 7.0 copy-start.28
  2882.2 7.6 copy-start.26
  2882.2 7.6 copy-start.37
  2882.2 7.6 copy-start.46
  2889.2 41.7 %copy-start.61 = (f32[256]{0:T(256)S(1)}, f32[256]{0:T(256)}, u32[]{:S(2)}) copy-start(f32[256]{0:T(256)} %copy-done.60) | copy-start | bytes 3076
  (32 other events, 118.6 us)
Sparse Core Ops, SparseCore 0:
  11.9 31.9 all-gather.4
  46.3 30.9 all-gather.2
  2781.5 32.3 reduce-scatter.8
  2817.4 30.8 reduce-scatter.6
  2851.7 77.2 reduce-scatter.12
  2932.3 76.4 reduce-scatter.10
  3015.6 191.1 all-reduce.5
where the time goes:
time: 3230 us; the launch traced here: 3220 us
  local copies, waits for them, and re-layouts  2660 us (82%)
  waiting for transfers between devices  279 us (9%)
  matrix products  124 us (4%)
  blocking collectives  109 us (3%)
    gather x3, local copies, waits for them, and re-layouts, on_device(): bucket_map = buckets[offsets]  2560 us
    psum x1, waiting for transfers between devices, on_device(): lax.psum((grad_query, grad_key, grad_value, grad_output, grad_gain_attn,...  195 us
    reduce_scatter x1, waiting for transfers between devices, on_device(): lax.psum_scatter(whole_out.astype(jnp.bfloat16), ('context', 'dp'), scatt...  70.2 us
  transfers between devices with their start and end apart: 8, of which 3 were waited for; matrix products, arithmetic and copies ran while one was open for 85% of the time, Pallas kernels for 0%

commit v1 on v0

v1 whole, which is shorter than its diff:
```python
import functools

import jax
import jax.numpy as jnp
from jax import lax
from jax.experimental import pallas as pl
from jax.experimental.pallas import tpu as pltpu
from jax.sharding import PartitionSpec as P

SINGLE = jnp.float32
BFLOAT = jnp.bfloat16
NT = (((1,), (1,)), ((), ()))
TN = (((0,), (0,)), ((), ()))


def rms_scale(value_rows, gain):
    return (
        value_rows
        * lax.rsqrt(jnp.mean(value_rows * value_rows, axis=-1, keepdims=True) + 1e-06)
        * gain
    )


def mm(left, right, dims=(((1,), (0,)), ((), ()))):
    return lax.dot_general(left, right, dims, preferred_element_type=SINGLE)


def lane_mask(shape, part, head_dim):
    return lax.broadcasted_iota(jnp.int32, shape, 1) // head_dim == part


def biased_scores(query, key, window_row):
    rows, cols = query.shape[0], key.shape[0]
    width = window_row.shape[1]
    spread = jnp.broadcast_to(window_row, (rows, width))
    shifted = pltpu.roll(spread, width - rows + 1, 1, stride=1, stride_axis=0)
    return mm(query, key, NT) + shifted[:, :cols]


def attend_kernel(head_dim, q_ref, k_ref, v_ref, win_ref, o_ref, lse_ref):
    query, key, value = q_ref[...], k_ref[...], v_ref[...]
    total = jnp.zeros(query.shape, SINGLE)
    for part in range(query.shape[1] // head_dim):
        mask = lane_mask(query.shape, part, head_dim)
        scores = biased_scores(jnp.where(mask, query, 0), key, win_ref[part])
        top = jnp.max(scores, axis=-1, keepdims=True)
        raised = jnp.exp(scores - top)
        summed = jnp.sum(raised, axis=-1, keepdims=True)
        lse_ref[part] = top + jnp.log(summed)
        probs = (raised * (1.0 / summed)).astype(BFLOAT)
        total = jnp.where(mask, mm(probs, value), total)
    o_ref[...] = total.astype(BFLOAT)


def attend_back_kernel(
    head_dim, q_ref, k_ref, v_ref, do_ref, lse_ref, win_ref, dq_ref, dkv_ref, diag_ref
):
    query, key, value, grad = q_ref[...], k_ref[...], v_ref[...], do_ref[...]
    rows, cols = query.shape[0], key.shape[0]
    blocks = cols // rows
    grad_q = jnp.zeros(query.shape, SINGLE)
    grad_k = jnp.zeros(key.shape, SINGLE)
    grad_v = jnp.zeros(key.shape, SINGLE)
    flip = (
        lax.broadcasted_iota(jnp.int32, (rows, rows), 0)
        + lax.broadcasted_iota(jnp.int32, (rows, rows), 1)
        == rows - 1
    ).astype(SINGLE).astype(BFLOAT)
    for part in range(query.shape[1] // head_dim):
        mask = lane_mask(query.shape, part, head_dim)
        mask_k = lane_mask(key.shape, part, head_dim)
        scores = biased_scores(jnp.where(mask, query, 0), key, win_ref[part])
        probs = jnp.exp(scores - lse_ref[part])
        grad_probs = mm(jnp.where(mask, grad, 0), value, NT)
        inner = jnp.sum(probs * grad_probs, axis=-1, keepdims=True)
        grad_scores = (probs * (grad_probs - inner)).astype(BFLOAT)
        grad_q = jnp.where(mask, mm(grad_scores, key), grad_q)
        grad_k = jnp.where(mask_k, mm(grad_scores, query, TN), grad_k)
        grad_v = jnp.where(mask_k, mm(probs.astype(BFLOAT), grad, TN), grad_v)
        turned = jnp.concatenate(
            [mm(flip, grad_scores), jnp.zeros((rows, rows), SINGLE)], axis=1
        )
        lined = pltpu.roll(turned, 0, 1, stride=1, stride_axis=0)
        diag_ref[part] = jnp.sum(lined, axis=0, keepdims=True)
    dq_ref[...] = grad_q.astype(BFLOAT)
    grad_k, grad_v = grad_k.astype(BFLOAT), grad_v.astype(BFLOAT)
    for block in range(blocks):
        dkv_ref[block, 0] = grad_k[block * rows : (block + 1) * rows]
        dkv_ref[block, 1] = grad_v[block * rows : (block + 1) * rows]


def attention_specs(rows, cols, lanes, parts, pairs, span):
    return dict(
        q=pl.BlockSpec((rows, lanes), lambda p: (0, p)),
        k=pl.BlockSpec((cols, lanes), lambda p: (0, p)),
        v=pl.BlockSpec((cols, lanes), lambda p: (0, p + pairs)),
        win=pl.BlockSpec((parts, 1, span), lambda p: (p, 0, 0)),
        lse=pl.BlockSpec((parts, rows, 1), lambda p: (p, 0, 0)),
    )


def attend(query, pair_all, window, head_dim):
    rows, width = query.shape
    cols, heads, span = pair_all.shape[0], window.shape[0], window.shape[2]
    lanes = max(128, head_dim)
    pairs, parts = width // lanes, lanes // head_dim
    spec = attention_specs(rows, cols, lanes, parts, pairs, span)
    return pl.pallas_call(
        functools.partial(attend_kernel, head_dim),
        grid=(pairs,),
        in_specs=[spec["q"], spec["k"], spec["v"], spec["win"]],
        out_specs=[spec["q"], spec["lse"]],
        out_shape=[
            jax.ShapeDtypeStruct((rows, width), BFLOAT),
            jax.ShapeDtypeStruct((heads, rows, 1), SINGLE),
        ],
        compiler_params=pltpu.CompilerParams(vmem_limit_bytes=40 * 2**20),
        cost_estimate=pl.CostEstimate(
            flops=4 * rows * cols * width,
            bytes_accessed=4 * cols * width + 4 * rows * width,
            transcendentals=heads * rows * cols,
        ),
    )(query, pair_all, pair_all, window)


def attend_back(query, pair_all, grad, lse, window, head_dim):
    rows, width = query.shape
    cols, heads, span = pair_all.shape[0], window.shape[0], window.shape[2]
    lanes = max(128, head_dim)
    pairs, parts = width // lanes, lanes // head_dim
    spec = attention_specs(rows, cols, lanes, parts, pairs, span)
    blocks = cols // rows
    return pl.pallas_call(
        functools.partial(attend_back_kernel, head_dim),
        grid=(pairs,),
        in_specs=[spec["q"], spec["k"], spec["v"], spec["q"], spec["lse"], spec["win"]],
        out_specs=[
            spec["q"],
            pl.BlockSpec((blocks, 2, rows, lanes), lambda p: (0, 0, 0, p)),
            spec["win"],
        ],
        out_shape=[
            jax.ShapeDtypeStruct((rows, width), BFLOAT),
            jax.ShapeDtypeStruct((blocks, 2, rows, width), BFLOAT),
            jax.ShapeDtypeStruct((heads, 1, span), SINGLE),
        ],
        compiler_params=pltpu.CompilerParams(vmem_limit_bytes=48 * 2**20),
        cost_estimate=pl.CostEstimate(
            flops=12 * rows * cols * width,
            bytes_accessed=8 * cols * width + 8 * rows * width,
            transcendentals=heads * rows * cols,
        ),
    )(query, pair_all, pair_all, grad, lse, window)


def weight_kernel(rows_ref, pre_ref, act_ref, grad_ref, in_ref, out_ref):
    in_ref[0, 0] = mm(rows_ref[0], pre_ref[0], TN).astype(BFLOAT)
    out_ref[0, 0] = mm(act_ref[0], grad_ref[0], TN).astype(BFLOAT)


def weight_grads(rows, grad_pre, act, grad, shares):
    experts, count, width = rows.shape
    hidden = act.shape[2]
    share = hidden // shares
    whole = pl.BlockSpec((1, count, width), lambda e, s: (e, 0, 0))
    part = pl.BlockSpec((1, count, share), lambda e, s: (e, 0, s))
    return pl.pallas_call(
        weight_kernel,
        grid=(experts, shares),
        in_specs=[whole, part, part, whole],
        out_specs=[
            pl.BlockSpec((1, 1, width, share), lambda e, s: (s, e, 0, 0)),
            pl.BlockSpec((1, 1, share, width), lambda e, s: (s, e, 0, 0)),
        ],
        out_shape=[
            jax.ShapeDtypeStruct((shares, experts, width, share), BFLOAT),
            jax.ShapeDtypeStruct((shares, experts, share, width), BFLOAT),
        ],
        compiler_params=pltpu.CompilerParams(vmem_limit_bytes=32 * 2**20),
        cost_estimate=pl.CostEstimate(
            flops=4 * experts * count * width * hidden,
            bytes_accessed=4 * experts * width * hidden,
            transcendentals=0,
        ),
    )(rows, grad_pre, act, grad)


def on_device(
    tokens,
    cotangent,
    w_query,
    w_key,
    w_value,
    w_output,
    gain_attn,
    gain_ffn,
    bias_table,
    w_router,
    w_in,
    w_out,
    routes,
    slots,
    buckets,
):
    tok_count = tokens.shape[1]
    width = tokens.shape[2]
    heads = bias_table.shape[1]
    bucket_count = bias_table.shape[0]
    head_dim = width // heads
    n_context = lax.axis_size("context")
    seq_len = tok_count * n_context
    n_owner = lax.axis_size("experts")
    shares = n_context * lax.axis_size("dp")
    expert_dev = w_in.shape[0]
    capacity = 2 * tok_count // (expert_dev * n_owner)
    highest = lax.Precision.HIGHEST
    resid = tokens[0].astype(SINGLE)
    first_norm_output = rms_scale(resid, gain_attn).astype(BFLOAT)
    pair_bf = jnp.concatenate(
        [mm(first_norm_output, w_key).astype(BFLOAT), mm(first_norm_output, w_value).astype(BFLOAT)],
        axis=1,
    )
    pair_all = lax.all_gather(pair_bf, "context", axis=0, tiled=True)
    query_bf = mm(first_norm_output, w_query).astype(BFLOAT)
    span = seq_len + tok_count
    first = seq_len - (lax.axis_index("context") + 1) * tok_count
    bucket_window = lax.dynamic_slice(jnp.pad(buckets, (0, 1)), (first,), (span,))
    window_hot = (
        bucket_window[:, None] == jnp.arange(bucket_count, dtype=jnp.int32)[None, :]
    ).astype(SINGLE)
    window = jnp.einsum("ob,bh->ho", window_hot, bias_table, precision=highest)[:, None, :]
    attention_result, log_total = attend(query_bf, pair_all, window, head_dim)
    residual_middle = resid + mm(attention_result, w_output)
    norm_two = rms_scale(residual_middle, gain_ffn)
    logits = jnp.dot(norm_two, w_router, precision=highest)
    route_probs = jax.nn.softmax(logits, axis=-1)
    route_row = routes[0]
    slot_row = slots[0]
    route_hot = (
        route_row[:, None] == jnp.arange(logits.shape[1], dtype=jnp.int32)[None, :]
    ).astype(SINGLE)
    gate = jnp.sum(route_probs * route_hot, axis=-1)
    grad_out = cotangent[0].astype(SINGLE)
    grad_routed = (grad_out * gate[:, None]).astype(BFLOAT)
    slot_count = expert_dev * n_owner * capacity
    layout = (
        route_row // expert_dev * (expert_dev * capacity)
        + route_row % expert_dev * capacity
        + slot_row
    )
    place = jnp.where(slot_row < capacity, layout, -1)
    slot_hot = (place[:, None] == jnp.arange(slot_count, dtype=jnp.int32)[None, :]).astype(BFLOAT)
    send = mm(
        slot_hot, jnp.concatenate([norm_two.astype(BFLOAT), grad_routed], axis=1), TN
    ).astype(BFLOAT)
    arrived = lax.all_to_all(
        send.reshape(n_owner, expert_dev, capacity, 2 * width),
        "experts", split_axis=0, concat_axis=0, tiled=True,
    )
    arrived = arrived.transpose(1, 0, 2, 3).reshape(expert_dev, n_owner * capacity, 2 * width)
    rows, grad_expert = arrived[:, :, :width], arrived[:, :, width:]
    pre_act = jnp.einsum("erd,edf->erf", rows, w_in, preferred_element_type=SINGLE)
    act_bf = jax.nn.gelu(pre_act).astype(BFLOAT)
    expert_back = jnp.einsum("erf,efd->erd", act_bf, w_out, preferred_element_type=SINGLE).astype(
        BFLOAT
    )
    grad_act = jnp.einsum("erd,efd->erf", grad_expert, w_out, preferred_element_type=SINGLE)
    grad_pre = jax.vjp(jax.nn.gelu, pre_act)[1](grad_act)[0].astype(BFLOAT)
    grad_rows = jnp.einsum("erf,edf->erd", grad_pre, w_in, preferred_element_type=SINGLE).astype(
        BFLOAT
    )
    both_back = jnp.concatenate([expert_back, grad_rows], axis=2)
    both_back = both_back.reshape(expert_dev, n_owner, capacity, 2 * width).transpose(1, 0, 2, 3)
    returned = lax.all_to_all(
        both_back, "experts", split_axis=0, concat_axis=0, tiled=True
    ).reshape(slot_count, 2 * width)
    whole_in, whole_out = weight_grads(rows, grad_pre, act_bf, grad_expert, shares)
    grad_w_in = lax.psum_scatter(whole_in, ("context", "dp"), scatter_dimension=0, tiled=True)
    grad_w_out = lax.psum_scatter(whole_out, ("context", "dp"), scatter_dimension=0, tiled=True)
    fetched = mm(slot_hot, returned)
    routed = fetched[:, :width]
    output = residual_middle + gate[:, None] * routed
    grad_gate = jnp.sum(grad_out * routed, axis=-1)
    grad_logits = grad_gate[:, None] * route_probs * (route_hot - gate[:, None])
    grad_router = jnp.einsum("td,te->de", norm_two, grad_logits, precision=highest)
    grad_norm_two = fetched[:, width:] + jnp.einsum(
        "te,de->td", grad_logits, w_router, precision=highest
    )
    grad_mid, grad_gain_ffn = jax.vjp(rms_scale, residual_middle, gain_ffn)[1](grad_norm_two)
    grad_mid = grad_mid + grad_out
    grad_attn = grad_mid.astype(BFLOAT)
    grad_output = mm(attention_result, grad_attn, TN)
    grad_attended = mm(grad_attn, w_output, NT).astype(BFLOAT)
    grad_q, grad_pair, diagonal = attend_back(
        query_bf, pair_all, grad_attended, log_total, window, head_dim
    )
    grad_pair = lax.psum_scatter(grad_pair, "context", scatter_dimension=0, tiled=True)[0]
    grad_k, grad_v = grad_pair[0], grad_pair[1]
    grad_table = jnp.einsum("ho,ob->bh", diagonal[:, 0, :], window_hot, precision=highest)
    grad_query = mm(first_norm_output, grad_q, TN)
    grad_key = mm(first_norm_output, grad_k, TN)
    grad_value = mm(first_norm_output, grad_v, TN)
    grad_norm_one = mm(grad_q, w_query, NT) + mm(grad_k, w_key, NT) + mm(grad_v, w_value, NT)
    grad_resid, grad_gain_attn = jax.vjp(rms_scale, resid, gain_attn)[1](grad_norm_one)
    grad_tokens = grad_resid + grad_mid
    grads = (
        grad_query,
        grad_key,
        grad_value,
        grad_output,
        grad_gain_attn,
        grad_gain_ffn,
        grad_table,
        grad_router,
    )
    small = jnp.concatenate([grad.reshape(-1) for grad in grads[4:]])
    small_rows = -(-small.shape[0] // width // 16) * 16
    small = jnp.pad(small, (0, small_rows * width - small.shape[0])).reshape(small_rows, width)
    packed = jnp.concatenate([*grads[:4], small], axis=0).astype(BFLOAT)
    packed = lax.psum(packed, ("experts", "context", "dp")).astype(SINGLE)
    summed = [packed[at * width : (at + 1) * width] for at in range(4)]
    flat, at = packed[4 * width :].reshape(-1), 0
    for grad in grads[4:]:
        summed.append(flat[at : at + grad.size].reshape(grad.shape))
        at += grad.size
    return (
        output.astype(BFLOAT)[None],
        grad_tokens[None],
        summed[0],
        summed[1],
        summed[2],
        summed[3],
        summed[4],
        summed[5],
        summed[6],
        summed[7],
        grad_w_in[0].astype(SINGLE),
        grad_w_out[0].astype(SINGLE),
    )


def solution(mesh):
    in_specs = (
        P(("experts", "dp"), "context", None),
        P(("experts", "dp"), "context", None),
        P(),
        P(),
        P(),
        P(),
        P(),
        P(),
        P(),
        P(),
        P("experts", None, None),
        P("experts", None, None),
        P(("experts", "dp"), "context"),
        P(("experts", "dp"), "context"),
        P(),
    )
    out_specs = (
        P(("experts", "dp"), "context", None),
        P(("experts", "dp"), "context", None),
        P(),
        P(),
        P(),
        P(),
        P(),
        P(),
        P(),
        P(),
        P("experts", None, ("context", "dp")),
        P("experts", ("context", "dp"), None),
    )
    return jax.shard_map(
        on_device, mesh=mesh, in_specs=in_specs, out_specs=out_specs, check_vma=False
    )
```

time: 3230 us -> 626 us (0.19)
  local copies, waits for them, and re-layouts: 2660 us -> 25.3 us
  waiting for transfers between devices: 279 us -> 395 us
  matrix products: 124 us -> 55.5 us
  Pallas kernels: 0 us -> 40.3 us
    gather x7 -> x0, local copies, waits for them, and re-layouts: 2570 us -> none  [the longest x3 2560 us: on_device(): bucket_map = buckets[offsets]]
    unnamed x8 -> x6, waiting for transfers between devices: 0.12 us -> 82.5 us
    reduce_scatter x3 -> x2, waiting for transfers between devices: 70.2 us -> 149 us  [the longest x1 77.4 us: on_device(): lax.psum_scatter(whole_in, ('context', 'dp'), scatter_dimension=0, tiled=...]
    psum x1, waiting for transfers between devices: 195 us -> 120 us  [on_device(): packed = lax.psum(packed, ('experts', 'context', 'dp')).astype(SINGLE)]
    dot_general x26 -> x20, matrix products: 119 us -> 52.5 us  [the longest x14 22.3 us: mm(): return lax.dot_general(left, right, dims, preferred_element_type=SINGLE)]
    all_gather x2 -> x1, waiting for transfers between devices: 0.02 us -> 43.8 us  [on_device(): pair_all = lax.all_gather(pair_bf, 'context', axis=0, tiled=True)]
    psum x1 -> x0, blocking collectives: 40.4 us -> none  [on_device(): lax.psum((grad_query, grad_key, grad_value, grad_output, grad_gain_attn,...]
    pallas_call x0 -> x3, Pallas kernels: none -> 40.3 us  [the longest x1 18.1 us: attend_back(): pl.pallas_call(functools.partial(attend_back_kernel, head_dim), grid=(pai...]
  transfers between devices with their start and end apart: 8 -> 5, of which waited for: 3 -> 5; matrix products, arithmetic and copies ran while one was open for 85% -> 4% of each run, Pallas kernels for 0% -> 2%
where the time goes in v1:
time: 626 us; the launch traced here: 623 us
  waiting for transfers between devices  395 us (63%)
  blocking collectives  78.3 us (13%)
  matrix products  55.5 us (9%)
  Pallas kernels  40.3 us (6%)
  local copies, waits for them, and re-layouts  25.3 us (4%)
  other arithmetic  14.4 us (2%)
  between operations  14.3 us (2%)
    psum x1, waiting for transfers between devices, on_device(): packed = lax.psum(packed, ('experts', 'context', 'dp')).astype(SINGLE)  120 us
    unnamed x6, waiting for transfers between devices  82.5 us
    reduce_scatter x1, waiting for transfers between devices, on_device(): lax.psum_scatter(whole_in, ('context', 'dp'), scatter_dimension=0, tiled=...  77.4 us
    reduce_scatter x1, waiting for transfers between devices, on_device(): lax.psum_scatter(whole_out, ('context', 'dp'), scatter_dimension=0, tiled...  71.3 us
    all_gather x1, waiting for transfers between devices, on_device(): pair_all = lax.all_gather(pair_bf, 'context', axis=0, tiled=True)  43.8 us
    all_to_all x1, blocking collectives, on_device(): lax.all_to_all(send.reshape(n_owner, expert_dev, capacity, 2 * width), 'e...  39.3 us
    all_to_all x1, blocking collectives, on_device(): lax.all_to_all(both_back, 'experts', split_axis=0, concat_axis=0, tiled=T...  39 us
    dot_general x14, matrix products, mm(): return lax.dot_general(left, right, dims, preferred_element_type=SINGLE)  22.3 us
  transfers between devices with their start and end apart: 5, of which 5 were waited for; matrix products, arithmetic and copies ran while one was open for 4% of the time, Pallas kernels for 2%

profile of v1, /device:TPU:25, one launch (start us, length us, event | category | flops | bytes accessed | tf_op | source)
XLA Modules:
  0.0 623.5 jit_solution(9988458583059084053)
XLA Ops:
  7.2 1.2 fusion.19
  9.1 1.6 convolution_convert_fusion.8
  10.8 1.9 convolution_convert_fusion.9
  12.7 0.9 pad_maximum_fusion.1
  15.0 43.8 %all-gather.2.cloned.1.call-done.k_ref.v_ref = bf16[1024,1536]{1,0:T(8,128)(2,1)} async-done(((bf16[256,1536]{1,0:T(8,128)(2,1)}), bf16[1024,1536]{1,0:T(8,128)(2,1)}) %all-gather.2.cloned.1.call-update) | async-done | bytes 3145744 | tf_op jit(solution)/shard_map/all_gather | solution.py:223
  58.8 1.9 copy-done.1
  60.7 9.9 %shard_map.238 = (bf16[256,768]{1,0:T(8,128)(2,1)S(1)}, f32[12,256,1]{2,1,0:T(8,128)S(1)}) custom-call(bf16[256,768]{1,0:T(8,128)(2,1)S(1)} %convolution_convert_fusion.10.q_ref, bf16[1024,1536]{1,0:T(8,128)(2,1)S(1)} %copy-done.1, bf16[1024,1536]{1,0:T(8,128)(2,1)S(1)} %copy-done.1, f32[12,1,1280]{2,1,0:T(1,128)S(1)} %broadcast_in_dim.11.win_ref), custom_call_target="tpu_custom_call" | custom-call | flops 805306368 | bytes 3932160 | tf_op jit(solution)/shard_map/pallas_call | solution.py:108
  71.2 0.8 fusion.88
  72.3 0.7 convolution_convert_fusion
  73.0 39.3 %all_to_all.10 = bf16[4,2,64,1536]{3,2,1,0:T(8,128)(2,1)S(1)} all-to-all(bf16[4,2,64,1536]{3,2,1,0:T(8,128)(2,1)S(1)} %bitcast.110), channel_id=1, replica_groups=mesh['experts'=4,'context'=4,'dp'=2] {'experts'}, dimensions={0} | all-to-all | bytes 3145728 | tf_op jit(solution)/shard_map/all_to_all | solution.py:256
  112.5 5.7 multiply_convert_fusion
  118.2 9.8 %fusion.6.pre_ref = bf16[2,256,3072]{2,1,0:T(8,128)(2,1)S(1)} fusion(f32[2,256,3072]{2,1,0:T(8,128)} %get-tuple-element.69, bf16[2,3072,768]{2,1,0:T(8,128)(2,1)} %param.26, bf16[2,256,1536]{2,1,0:T(8,128)(2,1)S(1)} %bitcast.104), kind=kOutput, calls=%fused_computation.8 | convolution fusion | flops 2447376384 | bytes 19660800 | tf_op jit(solution)/shard_map/erd,efd->erf/dot_general | solution.py:267
  128.1 7.4 %convolution_convert_fusion.5 = bf16[2,256,768]{2,1,0:T(8,128)(2,1)S(1)} fusion(bf16[2,256,3072]{2,1,0:T(8,128)(2,1)S(1)} %fusion.6.pre_ref, bf16[2,768,3072]{2,1,0:T(8,128)(2,1)} %param.25), kind=kOutput, calls=%fused_computation.22 | convolution fusion | flops 2416312320 | bytes 13369344 | tf_op jit(solution)/shard_map/erf,edf->erd/dot_general | solution.py:269
  135.5 6.3 %convolution_convert_fusion.6 = bf16[2,256,768]{2,1,0:T(8,128)(2,1)S(1)} fusion(bf16[2,256,3072]{2,1,0:T(8,128)(2,1)S(1)} %get-tuple-element.68.act_ref, bf16[2,3072,768]{2,1,0:T(8,128)(2,1)} %param.26), kind=kOutput, calls=%fused_computation.23 | convolution fusion | flops 2416312320 | bytes 13369344 | tf_op jit(solution)/shard_map/erf,efd->erd/dot_general | solution.py:264
  142.1 39.0 %all_to_all.11 = bf16[4,2,64,1536]{3,2,1,0:T(8,128)(2,1)S(1)} all-to-all(bf16[4,2,64,1536]{3,2,1,0:T(8,128)(2,1)S(1)} %bitcast.109), channel_id=1, replica_groups=mesh['experts'=4,'context'=4,'dp'=2] {'experts'}, dimensions={0} | all-to-all | bytes 3145728 | tf_op jit(solution)/shard_map/all_to_all | solution.py:274
  181.1 0.6 fusion.32
  181.7 0.9 fusion.26
  182.6 1.6 multiply_reduce_fusion
  185.3 18.1 %shard_map.239 = (bf16[256,768]{1,0:T(8,128)(2,1)S(1)}, bf16[4,2,256,768]{3,2,1,0:T(8,128)(2,1)S(1)}, f32[12,1,1280]{2,1,0:T(1,128)S(1)}) custom-call(bf16[256,768]{1,0:T(8,128)(2,1)S(1)} %convolution_convert_fusion.10.q_ref, bf16[1024,1536]{1,0:T(8,128)(2,1)} %all-gather.2.cloned.1.call-done.k_ref.v_ref, ...), custom_call_target="tpu_custom_call" | custom-call | flops 2415919104 | bytes 7864320 | tf_op jit(solution)/shard_map/pallas_call | solution.py:133
  203.4 1.7 copy-done.3
  206.3 0.6 convolution_convert_fusion.11
  207.9 0.7 reshape.206
  208.6 1.6 fusion.10
  210.8 82.2 %all-reduce.8.cloned.1.call-done = bf16[4,2,256,768]{3,2,1,0:T(8,128)(2,1)} async-done(((bf16[4,2,256,768]{3,2,1,0:T(8,128)(2,1)}), bf16[4,2,256,768]{3,2,1,0:T(8,128)(2,1)}) %all-reduce.8.cloned.1.call-update) | async-done | bytes 3145744
  292.9 2.6 convolution_add_fusion.2
  295.6 2.9 fusion.18
  298.4 0.6 fusion.55
  299.1 1.4 reshape.208
  300.4 3.4 fusion.9
  303.8 3.3 fusion.8
  307.1 1.5 fusion.7
  309.3 1.6 fusion.87
  310.9 0.7 copy-done.5
  311.7 1.9 copy-done.7
  313.6 12.3 %shard_map.240 = (bf16[8,2,768,384]{3,2,1,0:T(8,128)(2,1)S(1)}, bf16[8,2,384,768]{3,2,1,0:T(8,128)(2,1)}) custom-call(bf16[2,256,768]{2,1,0:T(8,128)(2,1)S(1)} %get-tuple-element.61.rows_ref, bf16[2,256,3072]{2,1,0:T(8,128)(2,1)S(1)} %copy-done.7, bf16[2,256,3072]{2,1,0:T(8,128)(2,1)S(1)} %copy-done.5, bf16[2,256,768]{2,1,0:T(8,128)(2,1)S(1)} %get-tuple-element.60.grad_ref), custom_call_target="tpu_custom_call" | custom-call | flops 4831838208 | bytes 18874368 | tf_op jit(solution)/shard_map/pallas_call | solution.py:167
  325.9 3.7 copy-done.2
  330.6 1.1 fusion.24
  331.7 119.9 %all-reduce.6.cloned.1.call-done = bf16[3088,768]{1,0:T(8,128)(2,1)} async-done(((bf16[3088,768]{1,0:T(8,128)(2,1)}), bf16[3088,768]{1,0:T(8,128)(2,1)}) %all-reduce.6.cloned.1.call-update) | async-done | bytes 4743184 | tf_op jit(solution)/shard_map/psum | solution.py:320
  451.6 0.7 slice.90
  453.4 0.7 copy.41
  454.1 0.7 copy.40
  454.8 3.2 convert_element_type.109
  458.0 0.6 slice_reduce_fusion
  458.6 3.8 fusion.86
  462.5 71.3 %reduce-scatter.5.cloned.1.call-done = bf16[1,2,384,768]{3,2,1,0:T(8,128)(2,1)} async-done(((bf16[8,2,384,768]{3,2,1,0:T(8,128)(2,1)}), bf16[1,2,384,768]{3,2,1,0:T(8,128)(2,1)}) %reduce-scatter.5.cloned.1.call-update) | async-done | bytes 1179664 | tf_op jit(solution)/shard_map/reduce_scatter | solution.py:279
  533.8 2.8 bitcast_convert_fusion
  536.7 77.4 %reduce-scatter.3.cloned.1.call-done = bf16[1,2,768,384]{3,2,1,0:T(8,128)(2,1)} async-done(((bf16[8,2,768,384]{3,2,1,0:T(8,128)(2,1)}), bf16[1,2,768,384]{3,2,1,0:T(8,128)(2,1)}) %reduce-scatter.3.cloned.1.call-update) | async-done | bytes 1179664 | tf_op jit(solution)/shard_map/reduce_scatter | solution.py:278
  614.1 2.8 bitcast_convert_fusion.1
  (109 shorter events, 9.6 us)
Async XLA Ops:
  7.2 1.9 copy-start
  7.2 51.6 %all-gather.2.cloned.1.call-start = ((), (), s32[]{:S(2)}) async-start(), calls=%async_computation.4 | async-start | bytes 3932160 | tf_op jit(solution)/shard_map/all_gather | solution.py:223
  8.5 0.6 copy-start.22
  9.0 199.6 %copy-start.24 = (f32[256]{0:T(256)}, f32[256]{0:T(256)S(1)}, u32[]{:S(2)}) copy-start(f32[256]{0:T(256)S(1)} %fusion.67) | copy-start | bytes 3076
  9.1 4.7 copy-start.27
  9.1 4.8 copy-start.33
  9.1 5.3 copy-start.20
  9.1 5.3 copy-start.31
  9.1 5.3 copy-start.11
  9.1 5.3 copy-start.15
  9.1 5.3 copy-start.21
  13.7 279.3 %all-reduce.8.cloned.1.call-start = ((), (), s32[]{:S(2)}) async-start(), calls=%async_computation.8 | async-start | bytes 6291456
  58.8 1.9 copy-start.1
  60.7 9.9 %copy-start.13 = (bf16[768,768]{1,0:T(8,128)(2,1)S(1)}, bf16[768,768]{1,0:T(8,128)(2,1)}, u32[]{:S(2)}) copy-start(bf16[768,768]{1,0:T(8,128)(2,1)} %param.20) | copy-start | bytes 3538948
  60.7 10.5 %copy-start.17 = (f32[768]{0:T(1024)S(1)}, f32[768]{0:T(1024)}, u32[]{:S(2)}) copy-start(f32[768]{0:T(1024)} %param.22) | copy-start | bytes 9220
  60.7 10.5 %copy-start.18 = (f32[768,8]{0,1:T(8,128)S(1)}, f32[768,8]{0,1:T(8,128)}, u32[]{:S(2)}) copy-start(f32[768,8]{0,1:T(8,128)} %param.24) | copy-start | bytes 73732
  70.6 1.5 copy-start.14
  72.1 40.3 %copy-start.32 = (bf16[2,768,3072]{2,1,0:T(8,128)(2,1)S(1)}, bf16[2,768,3072]{2,1,0:T(8,128)(2,1)}, u32[]{:S(2)}) copy-start(bf16[2,768,3072]{2,1,0:T(8,128)(2,1)} %param.25) | copy-start | bytes 28311556
  112.4 5.8 copy-start.10
  118.2 17.3 %copy-start.4 = (bf16[2,256,3072]{2,1,0:T(8,128)(2,1)}, bf16[2,256,3072]{2,1,0:T(8,128)(2,1)S(1)}, u32[]{:S(2)}) copy-start(bf16[2,256,3072]{2,1,0:T(8,128)(2,1)S(1)} %get-tuple-element.68.act_ref) | copy-start | bytes 9437188
  128.1 7.5 %copy-start.6 = (bf16[2,256,3072]{2,1,0:T(8,128)(2,1)}, bf16[2,256,3072]{2,1,0:T(8,128)(2,1)S(1)}, u32[]{:S(2)}) copy-start(bf16[2,256,3072]{2,1,0:T(8,128)(2,1)S(1)} %fusion.6.pre_ref) | copy-start | bytes 9437188
  184.4 0.9 copy-start.8
  203.4 1.7 copy-start.3
  205.1 0.7 copy-start.34
  205.1 3.5 copy-start.12
  205.1 246.4 %all-reduce.6.cloned.1.call-start = ((), (), s32[]{:S(2)}) async-start(), calls=%async_computation.5 | async-start | bytes 9486336 | tf_op jit(solution)/shard_map/psum | solution.py:320
  208.6 1.7 copy-start.16
  292.9 2.6 copy-start.25
  292.9 5.5 copy-start.28
  292.9 5.5 copy-start.29
  298.4 8.7 %copy-start.9 = (f32[256,768]{1,0:T(8,128)S(1)}, f32[256,768]{1,0:T(8,128)}, u32[]{:S(2)}) copy-start(f32[256,768]{1,0:T(8,128)} %copy-done.8) | copy-start | bytes 2359300
  300.4 8.2 %copy-start.19 = (bf16[16,768]{1,0:T(8,128)(2,1)S(1)}, bf16[16,768]{1,0:T(8,128)(2,1)}, u32[]{:S(2)}) copy-start(bf16[16,768]{1,0:T(8,128)(2,1)} %reshape.208) | copy-start | bytes 73732
  309.3 224.6 %reduce-scatter.5.cloned.1.call-start = ((), (), s32[]{:S(2)}) async-start(), calls=%async_computation.7 | async-start | bytes 10616832 | tf_op jit(solution)/shard_map/reduce_scatter | solution.py:279
  309.3 2.4 copy-start.5
  311.7 1.9 copy-start.7
  325.9 3.7 copy-start.2
  329.6 284.5 %reduce-scatter.3.cloned.1.call-start = ((), (), s32[]{:S(2)}) async-start(), calls=%async_computation.6 | async-start | bytes 10616832 | tf_op jit(solution)/shard_map/reduce_scatter | solution.py:278
  329.9 0.7 copy-start.23
  329.9 0.7 copy-start.30
  329.9 0.7 copy-start.26
  453.3 5.3 slice-start
  454.8 3.9 slice-start.1
Sparse Core Ops, SparseCore 0:
  13.8 44.9 all-gather.1
  205.3 87.6 all-reduce.7
  309.4 142.1 all-reduce.5
  455.3 78.4 reduce-scatter.4
  537.6 76.4 reduce-scatter.2

commit v2 on v1

--- a/solution.py
+++ b/solution.py
@@ -185,6 +185,219 @@
     )(rows, grad_pre, act, grad)
 
 
+MESH = pl.DeviceIdType.MESH
+ANY = pl.BlockSpec(memory_space=pl.ANY)
+VMEM = pl.BlockSpec(memory_space=pltpu.VMEM)
+
+
+def greet(peers):
+    barrier = pltpu.get_barrier_semaphore()
+    for peer in peers:
+        pl.semaphore_signal(barrier, inc=1, device_id=peer, device_id_type=MESH)
+    pl.semaphore_wait(barrier, len(peers))
+
+
+def remote(src, dst, send_sem, recv_sem, peer):
+    copy = pltpu.make_async_remote_copy(
+        src_ref=src,
+        dst_ref=dst,
+        send_sem=send_sem,
+        recv_sem=recv_sem,
+        device_id=peer,
+        device_id_type=MESH,
+    )
+    copy.start()
+    return copy
+
+
+def add_tiles(rows, own, others, store):
+    tile = 64 if rows % 64 == 0 else rows
+
+    def add(step, carry):
+        at = pl.ds(pl.multiple_of(step * tile, tile), tile)
+        total = own(step * tile, tile)
+        for other in others:
+            total = total + other[at].astype(SINGLE)
+        store(step * tile, tile, total)
+        return carry
+
+    lax.fori_loop(0, rows // tile, add, 0)
+
+
+def swap_kernel(axis, count, gather, x_ref, o_ref, send_sem, recv_sem, own_sem):
+    me = lax.axis_index(axis)
+    peers = [lax.rem(me + step, count) for step in range(1, count)]
+    greet([{axis: peer} for peer in peers])
+    copies = [
+        remote(
+            x_ref if gather else x_ref.at[peer],
+            o_ref.at[me],
+            send_sem.at[at],
+            recv_sem.at[at],
+            {axis: peer},
+        )
+        for at, peer in enumerate(peers)
+    ]
+    own = pltpu.make_async_copy(x_ref if gather else x_ref.at[me], o_ref.at[me], own_sem)
+    own.start()
+    own.wait()
+    for copy in copies:
+        copy.wait()
+
+
+def swap(x, axis, collective_id, gather=False):
+    count = lax.axis_size(axis)
+    shape = (count, *x.shape) if gather else x.shape
+    return pl.pallas_call(
+        functools.partial(swap_kernel, axis, count, gather),
+        in_specs=[ANY],
+        out_specs=ANY,
+        out_shape=jax.ShapeDtypeStruct(shape, x.dtype),
+        scratch_shapes=[
+            pltpu.SemaphoreType.DMA((count - 1,)),
+            pltpu.SemaphoreType.DMA((count - 1,)),
+            pltpu.SemaphoreType.DMA,
+        ],
+        compiler_params=pltpu.CompilerParams(collective_id=collective_id, has_side_effects=True),
+    )(x)
+
+
+def sum_kernel(axis, count, x_ref, o_ref, own, held, send_sem, recv_sem, own_sem):
+    me = lax.axis_index(axis)
+    peers = [lax.rem(me + step, count) for step in range(1, count)]
+    greet([{axis: peer} for peer in peers])
+    copies = [
+        remote(x_ref.at[peer], held.at[at], send_sem.at[at], recv_sem.at[at], {axis: peer})
+        for at, peer in enumerate(peers)
+    ]
+    mine = pltpu.make_async_copy(x_ref.at[me], own, own_sem)
+    mine.start()
+    mine.wait()
+    for copy in copies:
+        copy.wait()
+
+    def load(at, tile):
+        return own[pl.ds(pl.multiple_of(at, tile), tile)].astype(SINGLE)
+
+    def store(at, tile, total):
+        o_ref[pl.ds(pl.multiple_of(at, tile), tile)] = total.astype(BFLOAT)
+
+    add_tiles(own.shape[0], load, [held.at[at] for at in range(count - 1)], store)
+
+
+def sum_shares(x, axis, collective_id):
+    count, rows, width = x.shape
+    return pl.pallas_call(
+        functools.partial(sum_kernel, axis, count),
+        in_specs=[ANY],
+        out_specs=VMEM,
+        out_shape=jax.ShapeDtypeStruct((rows, width), x.dtype),
+        scratch_shapes=[
+            pltpu.VMEM((rows, width), x.dtype),
+            pltpu.VMEM((count - 1, rows, width), x.dtype),
+            pltpu.SemaphoreType.DMA((count - 1,)),
+            pltpu.SemaphoreType.DMA((count - 1,)),
+            pltpu.SemaphoreType.DMA,
+        ],
+        compiler_params=pltpu.CompilerParams(
+            collective_id=collective_id, has_side_effects=True, vmem_limit_bytes=24 * 2**20
+        ),
+    )(x)
+
+
+def reduce_kernel(orders, sizes, *refs):
+    count = len(orders)
+    x_refs, o_refs, scratch = refs[:count], refs[count : 2 * count], refs[2 * count :]
+    send_sem, recv_sem = scratch[-2:]
+    me = {axis: lax.axis_index(axis) for axis in sizes}
+    peers = {
+        axis: [lax.rem(me[axis] + step, size) for step in range(1, size)]
+        for axis, size in sizes.items()
+    }
+    greet([{axis: peer} for axis in sizes for peer in peers[axis]])
+    depth = len(sizes)
+    held = [scratch[2 * depth * at : 2 * depth * at + depth] for at in range(count)]
+    part = [scratch[2 * depth * at + depth : 2 * depth * (at + 1)] for at in range(count)]
+    chunks, places = [], []
+    for at, order in enumerate(orders):
+        rows, place, own_chunks, own_places = x_refs[at].shape[0], 0, [], []
+        for axis in order:
+            rows = rows // sizes[axis]
+            place = place + me[axis] * rows
+            own_chunks.append(rows)
+            own_places.append(place)
+        chunks.append(own_chunks)
+        places.append(own_places)
+
+    def begin(at, phase):
+        level = phase if phase < depth else 2 * depth - 1 - phase
+        axis, chunk = orders[at][level], chunks[at][level]
+        copies = []
+        for slot, peer in enumerate(peers[axis]):
+            if phase < depth:
+                source = x_refs[at] if level == 0 else part[at][level - 1]
+                src = source.at[pl.ds(pl.multiple_of(peer * chunk, chunk), chunk)]
+                dst = held[at][level].at[slot]
+            else:
+                where = pl.ds(pl.multiple_of(places[at][level], chunk), chunk)
+                src = dst = o_refs[at].at[where]
+            sems = send_sem.at[at, phase, slot], recv_sem.at[at, phase, slot]
+            copies.append(remote(src, dst, *sems, {axis: peer}))
+        return copies
+
+    def finish(at, phase, copies):
+        for copy in copies:
+            copy.wait()
+        if phase >= depth:
+            return
+        axis, chunk = orders[at][phase], chunks[at][phase]
+        source = x_refs[at] if phase == 0 else part[at][phase - 1]
+        last = phase == depth - 1
+        target = o_refs[at] if last else part[at][phase]
+        base = pl.multiple_of(places[at][phase], chunk) if last else 0
+        start = me[axis] * chunk
+
+        def load(row, tile):
+            return source[pl.ds(pl.multiple_of(start + row, tile), tile)].astype(SINGLE)
+
+        def store(row, tile, total):
+            target[pl.ds(pl.multiple_of(base + row, tile), tile)] = total.astype(target.dtype)
+
+        add_tiles(chunk, load, [held[at][phase].at[slot] for slot in range(len(peers[axis]))], store)
+
+    flying = [None] * count
+    for phase in range(2 * depth + 1):
+        for at in range(count):
+            if phase > 0:
+                finish(at, phase - 1, flying[at])
+            if phase < 2 * depth:
+                flying[at] = begin(at, phase)
+
+
+def reduce_all(pieces, orders, collective_id):
+    sizes = {axis: lax.axis_size(axis) for axis in orders[0]}
+    scratch = []
+    for piece, order in zip(pieces, orders):
+        rows, width = piece.shape
+        held, part = [], []
+        for axis in order:
+            rows = rows // sizes[axis]
+            held.append(pltpu.VMEM((sizes[axis] - 1, rows, width), piece.dtype))
+            part.append(pltpu.VMEM((rows, width), piece.dtype))
+        scratch += held + part
+    sems = (len(pieces), 2 * len(sizes), max(sizes.values()) - 1)
+    return pl.pallas_call(
+        functools.partial(reduce_kernel, orders, sizes),
+        in_specs=[VMEM] * len(pieces),
+        out_specs=[VMEM] * len(pieces),
+        out_shape=[jax.ShapeDtypeStruct(piece.shape, piece.dtype) for piece in pieces],
+        scratch_shapes=scratch + [pltpu.SemaphoreType.DMA(sems), pltpu.SemaphoreType.DMA(sems)],
+        compiler_params=pltpu.CompilerParams(
+            collective_id=collective_id, has_side_effects=True, vmem_limit_bytes=48 * 2**20
+        ),
+    )(*pieces)
+
+
 def on_device(
     tokens,
     cotangent,
@@ -220,7 +433,7 @@
         [mm(first_norm_output, w_key).astype(BFLOAT), mm(first_norm_output, w_value).astype(BFLOAT)],
         axis=1,
     )
-    pair_all = lax.all_gather(pair_bf, "context", axis=0, tiled=True)
+    pair_all = swap(pair_bf, "context", 0, gather=True).reshape(seq_len, 2 * width)
     query_bf = mm(first_norm_output, w_query).astype(BFLOAT)
     span = seq_len + tok_count
     first = seq_len - (lax.axis_index("context") + 1) * tok_count
@@ -253,10 +466,8 @@
     send = mm(
         slot_hot, jnp.concatenate([norm_two.astype(BFLOAT), grad_routed], axis=1), TN
     ).astype(BFLOAT)
-    arrived = lax.all_to_all(
-        send.reshape(n_owner, expert_dev, capacity, 2 * width),
-        "experts", split_axis=0, concat_axis=0, tiled=True,
-    )
+    arrived = swap(send.reshape(n_owner, expert_dev * capacity, 2 * width), "experts", 1)
+    arrived = arrived.reshape(n_owner, expert_dev, capacity, 2 * width)
     arrived = arrived.transpose(1, 0, 2, 3).reshape(expert_dev, n_owner * capacity, 2 * width)
     rows, grad_expert = arrived[:, :, :width], arrived[:, :, width:]
     pre_act = jnp.einsum("erd,edf->erf", rows, w_in, preferred_element_type=SINGLE)
@@ -271,10 +482,11 @@
     )
     both_back = jnp.concatenate([expert_back, grad_rows], axis=2)
     both_back = both_back.reshape(expert_dev, n_owner, capacity, 2 * width).transpose(1, 0, 2, 3)
-    returned = lax.all_to_all(
-        both_back, "experts", split_axis=0, concat_axis=0, tiled=True
+    whole_in, whole_out = weight_grads(rows, grad_pre, act_bf, grad_expert, shares)
+    both_back, whole_in, whole_out = lax.optimization_barrier((both_back, whole_in, whole_out))
+    returned = swap(
+        both_back.reshape(n_owner, expert_dev * capacity, 2 * width), "experts", 2
     ).reshape(slot_count, 2 * width)
-    whole_in, whole_out = weight_grads(rows, grad_pre, act_bf, grad_expert, shares)
     grad_w_in = lax.psum_scatter(whole_in, ("context", "dp"), scatter_dimension=0, tiled=True)
     grad_w_out = lax.psum_scatter(whole_out, ("context", "dp"), scatter_dimension=0, tiled=True)
     fetched = mm(slot_hot, returned)
@@ -294,8 +506,8 @@
     grad_q, grad_pair, diagonal = attend_back(
         query_bf, pair_all, grad_attended, log_total, window, head_dim
     )
-    grad_pair = lax.psum_scatter(grad_pair, "context", scatter_dimension=0, tiled=True)[0]
-    grad_k, grad_v = grad_pair[0], grad_pair[1]
+    grad_pair = sum_shares(grad_pair.reshape(n_context, 2 * tok_count, width), "context", 3)
+    grad_k, grad_v = grad_pair[:tok_count], grad_pair[tok_count:]
     grad_table = jnp.einsum("ho,ob->bh", diagonal[:, 0, :], window_hot, precision=highest)
     grad_query = mm(first_norm_output, grad_q, TN)
     grad_key = mm(first_norm_output, grad_k, TN)
@@ -313,13 +525,23 @@
         grad_table,
         grad_router,
     )
+    n_all = n_owner * shares
     small = jnp.concatenate([grad.reshape(-1) for grad in grads[4:]])
-    small_rows = -(-small.shape[0] // width // 16) * 16
-    small = jnp.pad(small, (0, small_rows * width - small.shape[0])).reshape(small_rows, width)
-    packed = jnp.concatenate([*grads[:4], small], axis=0).astype(BFLOAT)
-    packed = lax.psum(packed, ("experts", "context", "dp")).astype(SINGLE)
-    summed = [packed[at * width : (at + 1) * width] for at in range(4)]
-    flat, at = packed[4 * width :].reshape(-1), 0
+    small_rows = -(-small.shape[0] // (128 * 8 * n_all)) * 8 * n_all
+    small = jnp.pad(small, (0, small_rows * 128 - small.shape[0])).reshape(small_rows, 128)
+    unit = 16 * n_all
+    units = -(-4 * width // unit)
+    cut = -(-2 * units // 3) * unit
+    packed = jnp.concatenate([grad.astype(BFLOAT) for grad in grads[:4]], axis=0)
+    packed = jnp.pad(packed, ((0, units * unit - 4 * width), (0, 0)))
+    pieces, orders = [packed[:cut], small], [("dp", "context", "experts")] * 2
+    if cut < units * unit:
+        pieces.append(packed[cut:])
+        orders.append(("dp", "experts", "context"))
+    pieces = reduce_all(pieces, orders, 4)
+    packed = jnp.concatenate([pieces[0], *pieces[2:]], axis=0)
+    summed = [packed[at * width : (at + 1) * width].astype(SINGLE) for at in range(4)]
+    flat, at = pieces[1].reshape(-1), 0
     for grad in grads[4:]:
         summed.append(flat[at : at + grad.size].reshape(grad.shape))
         at += grad.size

time: 626 us -> 395 us (0.63)
  waiting for transfers between devices: 395 us -> 0.71 us
  Pallas kernels: 40.3 us -> 294 us
  blocking collectives: 78.3 us -> 0 us
  local copies, waits for them, and re-layouts: 25.3 us -> 14.3 us
  other arithmetic: 14.4 us -> 22.2 us
  matrix products: 55.5 us -> 49.1 us
    pallas_call x0 -> x5, Pallas kernels: none -> 253 us  [the longest x3 110 us: swap(): pl.pallas_call(functools.partial(swap_kernel, axis, count, gather), in_sp...]
    psum x1 -> x0, waiting for transfers between devices: 120 us -> none  [on_device(): packed = lax.psum(packed, ('experts', 'context', 'dp')).astype(SINGLE)]
    unnamed x6 -> x2, waiting for transfers between devices: 82.5 us -> 0.71 us
    all_to_all x2 -> x0, blocking collectives: 78.3 us -> none  [the longest x1 39.3 us: on_device(): lax.all_to_all(send.reshape(n_owner, expert_dev, capacity, 2 * width), 'e...]
    reduce_scatter x1, waiting for transfers between devices: 77.4 us -> 0.01 us  [on_device(): lax.psum_scatter(whole_in, ('context', 'dp'), scatter_dimension=0, tiled=...]
    reduce_scatter x1, waiting for transfers between devices: 71.3 us -> 0.01 us  [on_device(): lax.psum_scatter(whole_out, ('context', 'dp'), scatter_dimension=0, tiled...]
    all_gather x1 -> x0, waiting for transfers between devices: 43.8 us -> none  [on_device(): pair_all = lax.all_gather(pair_bf, 'context', axis=0, tiled=True)]
    dot_general x14, matrix products: 22.3 us -> 15.4 us  [mm(): return lax.dot_general(left, right, dims, preferred_element_type=SINGLE)]
  transfers between devices with their start and end apart: 5 -> 2, of which waited for: 5 -> 0; matrix products, arithmetic and copies ran while one was open for 4% -> 9% of each run, Pallas kernels for 2% -> 50%
where the time goes in v2:
time: 395 us
  Pallas kernels  294 us (74%)
  matrix products  49.1 us (12%)
  other arithmetic  22.2 us (6%)
  between operations  14.6 us (4%)
  local copies, waits for them, and re-layouts  14.3 us (4%)
    pallas_call x3, Pallas kernels, swap(): pl.pallas_call(functools.partial(swap_kernel, axis, count, gather), in_sp...  110 us
    pallas_call x1, Pallas kernels, reduce_all(): pl.pallas_call(functools.partial(reduce_kernel, orders, sizes), in_specs=...  100 us
    pallas_call x1, Pallas kernels, sum_shares(): pl.pallas_call(functools.partial(sum_kernel, axis, count), in_specs=[ANY]...  42.8 us
    pallas_call x1, Pallas kernels, attend_back(): pl.pallas_call(functools.partial(attend_back_kernel, head_dim), grid=(pai...  18.1 us
    dot_general x14, matrix products, mm(): return lax.dot_general(left, right, dims, preferred_element_type=SINGLE)  15.4 us
    pallas_call x1, Pallas kernels, weight_grads(): pl.pallas_call(weight_kernel, grid=(experts, shares), in_specs=[whole, pa...  12.3 us
    pallas_call x1, Pallas kernels, attend(): pl.pallas_call(functools.partial(attend_kernel, head_dim), grid=(pairs,),...  9.88 us
    unnamed x42, local copies, waits for them, and re-layouts  8.63 us
  transfers between devices with their start and end apart: 2, of which 0 were waited for; matrix products, arithmetic and copies ran while one was open for 9% of the time, Pallas kernels for 50%

profile of v2, /device:TPU:25, one launch (start us, length us, event | category | flops | bytes accessed | tf_op | source)
XLA Modules:
  0.0 394.6 jit_solution(16894806089372866845)
XLA Ops:
  7.3 1.3 fusion.16
  8.6 0.8 pad_dynamic-slice_fusion
  9.4 1.2 convolution_bitcast_fusion
  10.6 1.9 convolution_convert_fusion.10.q_ref
  12.6 0.5 convolution_convert_fusion.9
  13.2 0.5 convolution_convert_fusion.8
  13.7 0.9 pad_maximum_fusion.5.x_ref
  14.6 37.6 %shard_map.238 = bf16[4,256,1536]{2,1,0:T(8,128)(2,1)} custom-call(bf16[256,1536]{1,0:T(8,128)(2,1)} %pad_maximum_fusion.5.x_ref), custom_call_target="tpu_custom_call" | custom-call | tf_op jit(solution)/shard_map/pallas_call | solution.py:251
  52.3 1.9 copy-done.1
  54.2 9.9 %shard_map.239 = (bf16[256,768]{1,0:T(8,128)(2,1)S(1)}, f32[12,256,1]{2,1,0:T(8,128)S(1)}) custom-call(bf16[256,768]{1,0:T(8,128)(2,1)S(1)} %convolution_convert_fusion.10.q_ref, bf16[1024,1536]{1,0:T(8,128)(2,1)S(1)} %bitcast.79, bf16[1024,1536]{1,0:T(8,128)(2,1)S(1)} %bitcast.80, f32[12,1,1280]{2,1,0:T(1,128)S(1)} %broadcast_in_dim.11.win_ref), custom_call_target="tpu_custom_call" | custom-call | flops 805306368 | bytes 3932160 | tf_op jit(solution)/shard_map/pallas_call | solution.py:108
  64.1 0.6 multiply_reduce_fusion.2
  65.0 0.8 fusion.75
  66.1 1.8 convolution_convert_fusion
  68.0 36.7 %shard_map.240 = bf16[4,128,1536]{2,1,0:T(8,128)(2,1)} custom-call(bf16[4,128,1536]{2,1,0:T(8,128)(2,1)} %bitcast.89), custom_call_target="tpu_custom_call" | custom-call | tf_op jit(solution)/shard_map/pallas_call | solution.py:251
  104.6 1.5 copy.31
  106.3 6.6 %multiply_convert_fusion = (bf16[2,256,3072]{2,1,0:T(8,128)(2,1)S(1)}, f32[2,256,3072]{2,1,0:T(8,128)S(1)}) fusion(bf16[2,768,3072]{2,1,0:T(8,128)(2,1)} %param.25, bf16[2,256,1536]{2,1,0:T(8,128)(2,1)S(1)} %bitcast.84), kind=kOutput, calls=%fused_computation.9 | convolution fusion | flops 2430074880 | bytes 19660800 | tf_op jit(solution)/shard_map/erd,edf->erf/dot_general | solution.py:473
  112.8 7.9 %fusion.6.pre_ref = bf16[2,256,3072]{2,1,0:T(8,128)(2,1)S(1)} fusion(f32[2,256,3072]{2,1,0:T(8,128)S(1)} %get-tuple-element.81, bf16[2,3072,768]{2,1,0:T(8,128)(2,1)} %param.26, bf16[2,256,1536]{2,1,0:T(8,128)(2,1)S(1)} %bitcast.85), kind=kOutput, calls=%fused_computation.8 | convolution fusion | flops 2447376384 | bytes 19660800 | tf_op jit(solution)/shard_map/erd,efd->erf/dot_general | solution.py:478
  120.7 6.3 %convolution_convert_fusion.5 = bf16[2,256,768]{2,1,0:T(8,128)(2,1)S(1)} fusion(bf16[2,256,3072]{2,1,0:T(8,128)(2,1)S(1)} %fusion.6.pre_ref, bf16[2,768,3072]{2,1,0:T(8,128)(2,1)} %param.25), kind=kOutput, calls=%fused_computation.26 | convolution fusion | flops 2416312320 | bytes 13369344 | tf_op jit(solution)/shard_map/erf,edf->erd/dot_general | solution.py:480
  127.0 6.3 %convolution_convert_fusion.6 = bf16[2,256,768]{2,1,0:T(8,128)(2,1)S(1)} fusion(bf16[2,256,3072]{2,1,0:T(8,128)(2,1)S(1)} %get-tuple-element.80.act_ref, bf16[2,3072,768]{2,1,0:T(8,128)(2,1)} %param.26), kind=kOutput, calls=%fused_computation.27 | convolution fusion | flops 2416312320 | bytes 13369344 | tf_op jit(solution)/shard_map/erf,efd->erd/dot_general | solution.py:475
  133.4 1.2 copy.45
  134.7 12.3 %shard_map.241 = (bf16[8,2,768,384]{3,2,1,0:T(8,128)(2,1)S(1)}, bf16[8,2,384,768]{3,2,1,0:T(8,128)(2,1)}) custom-call(bf16[2,256,768]{2,1,0:T(8,128)(2,1)S(1)} %get-tuple-element.73.rows_ref, bf16[2,256,3072]{2,1,0:T(8,128)(2,1)S(1)} %fusion.6.pre_ref, bf16[2,256,3072]{2,1,0:T(8,128)(2,1)S(1)} %get-tuple-element.80.act_ref, ...), custom_call_target="tpu_custom_call" | custom-call | flops 4831838208 | bytes 18874368 | tf_op jit(solution)/shard_map/pallas_call | solution.py:167
  146.9 3.6 copy-done.2
  150.6 0.7 reduce-scatter.3.cloned.1.call-update
  151.3 35.8 %shard_map.242 = bf16[4,128,1536]{2,1,0:T(8,128)(2,1)} custom-call(bf16[4,128,1536]{2,1,0:T(8,128)(2,1)} %bitcast.82), custom_call_target="tpu_custom_call" | custom-call | tf_op jit(solution)/shard_map/pallas_call | solution.py:251
  187.1 3.3 fusion.25
  190.4 2.1 fusion.15
  192.5 1.5 fusion.22
  194.2 2.5 multiply_reduce_fusion
  196.8 1.5 convert_add_fusion.1
  199.2 18.1 %shard_map.243 = (bf16[256,768]{1,0:T(8,128)(2,1)S(1)}, bf16[4,2,256,768]{3,2,1,0:T(8,128)(2,1)S(1)}, f32[12,1,1280]{2,1,0:T(1,128)S(1)}) custom-call(bf16[256,768]{1,0:T(8,128)(2,1)S(1)} %convolution_convert_fusion.10.q_ref, bf16[1024,1536]{1,0:T(8,128)(2,1)} %bitcast.77, bf16[1024,1536]{1,0:T(8,128)(2,1)} %bitcast.78, ...), custom_call_target="tpu_custom_call" | custom-call | flops 2415919104 | bytes 7864320 | tf_op jit(solution)/shard_map/pallas_call | solution.py:133
  217.3 42.8 %shard_map.244 = bf16[512,768]{1,0:T(8,128)(2,1)S(1)} custom-call(bf16[4,512,768]{2,1,0:T(8,128)(2,1)S(1)} %bitcast.81), custom_call_target="tpu_custom_call" | custom-call | tf_op jit(solution)/shard_map/pallas_call | solution.py:290
  260.1 0.7 fusion.35
  260.9 1.9 fusion.76
  263.4 1.4 fusion.11
  264.9 0.6 convolution_convert_fusion.2
  265.5 0.5 convolution_convert_fusion.1
  266.1 0.6 convolution_convert_fusion.4
  266.7 0.6 convolution_convert_fusion.3
  267.3 2.0 pad_maximum_fusion.refs_0_
  269.4 100.4 %shard_map.245 = (bf16[2048,768]{1,0:T(8,128)(2,1)}, f32[256,128]{1,0:T(8,128)S(1)}, bf16[1024,768]{1,0:T(8,128)(2,1)S(1)}) custom-call(bf16[2048,768]{1,0:T(8,128)(2,1)} %pad_maximum_fusion.refs_0_, f32[256,128]{1,0:T(8,128)S(1)} %fusion.43.refs_1_, bf16[1024,768]{1,0:T(8,128)(2,1)S(1)} %pad_maximum_fusion.2.refs_2_), custom_call_target="tpu_custom_call" | custom-call | tf_op jit(solution)/shard_map/pallas_call | solution.py:389
  369.9 0.7 copy.35
  370.6 1.0 reshape.197
  371.6 1.7 copy.36
  373.3 0.6 slice_bitcast_fusion
  373.9 2.5 fusion.13
  376.4 5.7 %fusion.7 = (f32[768,768]{1,0:T(8,128)}, f32[768,768]{1,0:T(8,128)}, f32[768,768]{1,0:T(8,128)}, f32[768,768]{1,0:T(8,128)}) fusion(bf16[1024,768]{1,0:T(8,128)(2,1)S(1)} %get-tuple-element.34, bf16[2048,768]{1,0:T(8,128)(2,1)} %get-tuple-element.33), kind=kLoop, calls=%fused_computation.41 | loop fusion | flops 4128768 | bytes 17694720 | tf_op jit(solution)/shard_map/convert_element_type | solution.py:543
  382.1 2.8 bitcast_convert_fusion
  385.0 2.8 bitcast_convert_fusion.1
  (63 shorter events, 2.9 us)
Async XLA Ops:
  7.2 6.0 %copy-start = (bf16[768,768]{1,0:T(8,128)(2,1)S(1)}, bf16[768,768]{1,0:T(8,128)(2,1)}, u32[]{:S(2)}) copy-start(bf16[768,768]{1,0:T(8,128)(2,1)} %param.19) | copy-start | bytes 3538948
  7.2 5.4 %copy-start.9 = (bf16[1,256,768]{2,1,0:T(8,128)(2,1)S(1)}, bf16[1,256,768]{2,1,0:T(8,128)(2,1)}, u32[]{:S(2)}) copy-start(bf16[1,256,768]{2,1,0:T(8,128)(2,1)} %param.15) | copy-start | bytes 1179652
  7.2 5.4 %copy-start.17 = (f32[768]{0:T(1024)S(1)}, f32[768]{0:T(1024)}, u32[]{:S(2)}) copy-start(f32[768]{0:T(1024)} %param.21) | copy-start | bytes 9220
  7.2 5.4 %copy-start.13 = (bf16[768,768]{1,0:T(8,128)(2,1)S(1)}, bf16[768,768]{1,0:T(8,128)(2,1)}, u32[]{:S(2)}) copy-start(bf16[768,768]{1,0:T(8,128)(2,1)} %param.18) | copy-start | bytes 3538948
  7.2 374.9 %reduce-scatter.5.cloned.1.call-start = ((), (), s32[]{:S(2)}) async-start(), calls=%async_computation.3 | async-start | bytes 10616832 | tf_op jit(solution)/shard_map/reduce_scatter | solution.py:491
  52.3 1.9 copy-start.1
  54.2 10.0 %copy-start.10 = (bf16[768,768]{1,0:T(8,128)(2,1)S(1)}, bf16[768,768]{1,0:T(8,128)(2,1)}, u32[]{:S(2)}) copy-start(bf16[768,768]{1,0:T(8,128)(2,1)} %param.20) | copy-start | bytes 3538948
  64.0 2.1 copy-start.3
  64.1 0.7 copy-start.18
  64.1 0.8 copy-start.19
  64.1 0.8 copy-start.15
  64.1 0.9 copy-start.16
  64.1 1.8 copy-start.12
  64.7 1.4 copy-start.5
  146.9 3.6 copy-start.2
  150.6 234.4 %reduce-scatter.3.cloned.1.call-start = ((), (), s32[]{:S(2)}) async-start(), calls=%async_computation.2 | async-start | bytes 10616832 | tf_op jit(solution)/shard_map/reduce_scatter | solution.py:490
  187.1 3.3 copy-start.6
  194.2 4.1 %copy-start.11 = (bf16[768,768]{1,0:T(8,128)(2,1)S(1)}, bf16[768,768]{1,0:T(8,128)(2,1)}, u32[]{:S(2)}) copy-start(bf16[768,768]{1,0:T(8,128)(2,1)} %param.20) | copy-start | bytes 3538948
  196.8 2.4 copy-start.4
  198.3 0.9 copy-start.7
  260.9 1.9 copy-start.14
  263.4 2.1 copy-start.8
Sparse Core Ops, SparseCore 0:
  150.7 99.6 reduce-scatter.4
  253.9 110.3 reduce-scatter.2

commit v3 on v2

--- a/solution.py
+++ b/solution.py
@@ -153,38 +153,6 @@
     )(query, pair_all, pair_all, grad, lse, window)
 
 
-def weight_kernel(rows_ref, pre_ref, act_ref, grad_ref, in_ref, out_ref):
-    in_ref[0, 0] = mm(rows_ref[0], pre_ref[0], TN).astype(BFLOAT)
-    out_ref[0, 0] = mm(act_ref[0], grad_ref[0], TN).astype(BFLOAT)
-
-
-def weight_grads(rows, grad_pre, act, grad, shares):
-    experts, count, width = rows.shape
-    hidden = act.shape[2]
-    share = hidden // shares
-    whole = pl.BlockSpec((1, count, width), lambda e, s: (e, 0, 0))
-    part = pl.BlockSpec((1, count, share), lambda e, s: (e, 0, s))
-    return pl.pallas_call(
-        weight_kernel,
-        grid=(experts, shares),
-        in_specs=[whole, part, part, whole],
-        out_specs=[
-            pl.BlockSpec((1, 1, width, share), lambda e, s: (s, e, 0, 0)),
-            pl.BlockSpec((1, 1, share, width), lambda e, s: (s, e, 0, 0)),
-        ],
-        out_shape=[
-            jax.ShapeDtypeStruct((shares, experts, width, share), BFLOAT),
-            jax.ShapeDtypeStruct((shares, experts, share, width), BFLOAT),
-        ],
-        compiler_params=pltpu.CompilerParams(vmem_limit_bytes=32 * 2**20),
-        cost_estimate=pl.CostEstimate(
-            flops=4 * experts * count * width * hidden,
-            bytes_accessed=4 * experts * width * hidden,
-            transcendentals=0,
-        ),
-    )(rows, grad_pre, act, grad)
-
-
 MESH = pl.DeviceIdType.MESH
 ANY = pl.BlockSpec(memory_space=pl.ANY)
 VMEM = pl.BlockSpec(memory_space=pltpu.VMEM)
@@ -262,50 +230,7 @@
     )(x)
 
 
-def sum_kernel(axis, count, x_ref, o_ref, own, held, send_sem, recv_sem, own_sem):
-    me = lax.axis_index(axis)
-    peers = [lax.rem(me + step, count) for step in range(1, count)]
-    greet([{axis: peer} for peer in peers])
-    copies = [
-        remote(x_ref.at[peer], held.at[at], send_sem.at[at], recv_sem.at[at], {axis: peer})
-        for at, peer in enumerate(peers)
-    ]
-    mine = pltpu.make_async_copy(x_ref.at[me], own, own_sem)
-    mine.start()
-    mine.wait()
-    for copy in copies:
-        copy.wait()
-
-    def load(at, tile):
-        return own[pl.ds(pl.multiple_of(at, tile), tile)].astype(SINGLE)
-
-    def store(at, tile, total):
-        o_ref[pl.ds(pl.multiple_of(at, tile), tile)] = total.astype(BFLOAT)
-
-    add_tiles(own.shape[0], load, [held.at[at] for at in range(count - 1)], store)
-
-
-def sum_shares(x, axis, collective_id):
-    count, rows, width = x.shape
-    return pl.pallas_call(
-        functools.partial(sum_kernel, axis, count),
-        in_specs=[ANY],
-        out_specs=VMEM,
-        out_shape=jax.ShapeDtypeStruct((rows, width), x.dtype),
-        scratch_shapes=[
-            pltpu.VMEM((rows, width), x.dtype),
-            pltpu.VMEM((count - 1, rows, width), x.dtype),
-            pltpu.SemaphoreType.DMA((count - 1,)),
-            pltpu.SemaphoreType.DMA((count - 1,)),
-            pltpu.SemaphoreType.DMA,
-        ],
-        compiler_params=pltpu.CompilerParams(
-            collective_id=collective_id, has_side_effects=True, vmem_limit_bytes=24 * 2**20
-        ),
-    )(x)
-
-
-def reduce_kernel(orders, sizes, *refs):
+def reduce_kernel(orders, sizes, backs, *refs):
     count = len(orders)
     x_refs, o_refs, scratch = refs[:count], refs[count : 2 * count], refs[2 * count :]
     send_sem, recv_sem = scratch[-2:]
@@ -315,10 +240,11 @@
         for axis, size in sizes.items()
     }
     greet([{axis: peer} for axis in sizes for peer in peers[axis]])
-    depth = len(sizes)
-    held = [scratch[2 * depth * at : 2 * depth * at + depth] for at in range(count)]
-    part = [scratch[2 * depth * at + depth : 2 * depth * (at + 1)] for at in range(count)]
-    chunks, places = [], []
+    held, part, chunks, places, spot = [], [], [], [], 0
+    for order in orders:
+        held.append(scratch[spot : spot + len(order)])
+        part.append(scratch[spot + len(order) : spot + 2 * len(order)])
+        spot += 2 * len(order)
     for at, order in enumerate(orders):
         rows, place, own_chunks, own_places = x_refs[at].shape[0], 0, [], []
         for axis in order:
@@ -330,6 +256,7 @@
         places.append(own_places)
 
     def begin(at, phase):
+        depth = len(orders[at])
         level = phase if phase < depth else 2 * depth - 1 - phase
         axis, chunk = orders[at][level], chunks[at][level]
         copies = []
@@ -348,13 +275,14 @@
     def finish(at, phase, copies):
         for copy in copies:
             copy.wait()
+        depth = len(orders[at])
         if phase >= depth:
             return
         axis, chunk = orders[at][phase], chunks[at][phase]
         source = x_refs[at] if phase == 0 else part[at][phase - 1]
         last = phase == depth - 1
         target = o_refs[at] if last else part[at][phase]
-        base = pl.multiple_of(places[at][phase], chunk) if last else 0
+        base = pl.multiple_of(places[at][phase], chunk) if last and backs[at] else 0
         start = me[axis] * chunk
 
         def load(row, tile):
@@ -366,18 +294,19 @@
         add_tiles(chunk, load, [held[at][phase].at[slot] for slot in range(len(peers[axis]))], store)
 
     flying = [None] * count
-    for phase in range(2 * depth + 1):
+    phases = [len(order) * (2 if back else 1) for order, back in zip(orders, backs)]
+    for phase in range(max(phases) + 1):
         for at in range(count):
-            if phase > 0:
+            if 0 < phase <= phases[at]:
                 finish(at, phase - 1, flying[at])
-            if phase < 2 * depth:
+            if phase < phases[at]:
                 flying[at] = begin(at, phase)
 
 
-def reduce_all(pieces, orders, collective_id):
-    sizes = {axis: lax.axis_size(axis) for axis in orders[0]}
-    scratch = []
-    for piece, order in zip(pieces, orders):
+def reduce_all(pieces, orders, backs, collective_id):
+    sizes = {axis: lax.axis_size(axis) for order in orders for axis in order}
+    scratch, shapes = [], []
+    for piece, order, back in zip(pieces, orders, backs):
         rows, width = piece.shape
         held, part = [], []
         for axis in order:
@@ -385,17 +314,163 @@
             held.append(pltpu.VMEM((sizes[axis] - 1, rows, width), piece.dtype))
             part.append(pltpu.VMEM((rows, width), piece.dtype))
         scratch += held + part
+        shapes.append((piece.shape[0] if back else rows, width))
     sems = (len(pieces), 2 * len(sizes), max(sizes.values()) - 1)
     return pl.pallas_call(
-        functools.partial(reduce_kernel, orders, sizes),
+        functools.partial(reduce_kernel, orders, sizes, backs),
         in_specs=[VMEM] * len(pieces),
         out_specs=[VMEM] * len(pieces),
-        out_shape=[jax.ShapeDtypeStruct(piece.shape, piece.dtype) for piece in pieces],
+        out_shape=[
+            jax.ShapeDtypeStruct(shape, piece.dtype) for shape, piece in zip(shapes, pieces)
+        ],
         scratch_shapes=scratch + [pltpu.SemaphoreType.DMA(sems), pltpu.SemaphoreType.DMA(sems)],
         compiler_params=pltpu.CompilerParams(
             collective_id=collective_id, has_side_effects=True, vmem_limit_bytes=48 * 2**20
         ),
     )(*pieces)
+
+
+def pack(grads, unit):
+    packed = jnp.concatenate([grad.astype(BFLOAT) for grad in grads], axis=0)
+    return jnp.pad(packed, ((0, -packed.shape[0] % unit), (0, 0)))
+
+
+def gelu_both(pre):
+    root = 0.7978845608028654
+    square = pre * pre
+    bend = jnp.tanh(root * (pre + 0.044715 * square * pre))
+    half = 0.5 * (1.0 + bend)
+    slope = half + 0.5 * pre * (1.0 - bend * bend) * root * (1.0 + 0.134145 * square)
+    return pre * half, slope
+
+
+def expert_kernel(
+    axis, count, shares, x_ref, win_ref, wout_ref, back_ref, gin_ref, gout_ref,
+    arrived, leaving, w_in, w_out, act, grad_pre, total, grad_total, whole_in, whole_out,
+    send_sem, recv_sem, own_sem, load_sem, store_sem,
+):
+    experts, _, capacity, both = arrived.shape
+    width, hidden, rows = both // 2, w_in.shape[2], count * capacity
+    share = hidden // shares
+    me = lax.axis_index(axis)
+    peers = [lax.rem(me + step, count) for step in range(1, count)]
+    greet([{axis: peer} for peer in peers])
+    loads, coming = [], []
+    for e in range(experts):
+        here = [
+            remote(
+                x_ref.at[peer, e], arrived.at[e, me],
+                send_sem.at[0, e, at], recv_sem.at[0, e, at], {axis: peer},
+            )
+            for at, peer in enumerate(peers)
+        ]
+        own = pltpu.make_async_copy(x_ref.at[me, e], arrived.at[e, me], own_sem.at[0, e])
+        own.start()
+        coming.append(here + [own])
+    for e in range(experts):
+        pair = [
+            pltpu.make_async_copy(win_ref.at[e], w_in.at[e], load_sem.at[0, e]),
+            pltpu.make_async_copy(wout_ref.at[e], w_out.at[e], load_sem.at[1, e]),
+        ]
+        for copy in pair:
+            copy.start()
+        loads.append(pair)
+    tile = 512 if hidden % 512 == 0 else hidden
+    leave, stores = [], []
+    for e in range(experts):
+        for copy in coming[e] + loads[e]:
+            copy.wait()
+        landed = arrived[e].astype(SINGLE).reshape(rows, both).astype(BFLOAT)
+        came, grad = landed[:, :width], landed[:, width:]
+        total[...] = jnp.zeros_like(total)
+        grad_total[...] = jnp.zeros_like(grad_total)
+
+        def step(at, carry):
+            cut = pl.ds(pl.multiple_of(at * tile, tile), tile)
+            into, out = w_in[e, :, cut], w_out[e, cut, :]
+            value, slope = gelu_both(mm(came, into))
+            value = value.astype(BFLOAT)
+            act[:, cut] = value
+            total[...] += mm(value, out)
+            turned = (mm(grad, out, NT) * slope).astype(BFLOAT)
+            grad_pre[:, cut] = turned
+            grad_total[...] += mm(turned, into, NT)
+            return carry
+
+        lax.fori_loop(0, hidden // tile, step, 0)
+        leaving[e, :, :, :width] = total[...].reshape(count, capacity, width).astype(BFLOAT)
+        leaving[e, :, :, width:] = grad_total[...].reshape(count, capacity, width).astype(BFLOAT)
+        leave += [
+            remote(
+                leaving.at[e, peer], back_ref.at[me, e],
+                send_sem.at[1, e, at], recv_sem.at[1, e, at], {axis: peer},
+            )
+            for at, peer in enumerate(peers)
+        ]
+        own = pltpu.make_async_copy(leaving.at[e, me], back_ref.at[me, e], own_sem.at[1, e])
+        own.start()
+        leave.append(own)
+
+        def weigh(at, carry):
+            cut = pl.ds(pl.multiple_of(at * share, share), share)
+            whole_in[e, at] = mm(came, grad_pre[:, cut], TN).astype(BFLOAT)
+            whole_out[e, at] = mm(act[:, cut], grad, TN).astype(BFLOAT)
+            return carry
+
+        lax.fori_loop(0, shares, weigh, 0)
+        pair = [
+            pltpu.make_async_copy(whole_in.at[e], gin_ref.at[:, e], store_sem.at[0, e]),
+            pltpu.make_async_copy(whole_out.at[e], gout_ref.at[:, e], store_sem.at[1, e]),
+        ]
+        for copy in pair:
+            copy.start()
+        stores += pair
+    for copy in leave + stores:
+        copy.wait()
+
+
+def expert_layer(x, w_in, w_out, axis, shares, collective_id):
+    count, experts, capacity, both = x.shape
+    width, hidden = w_in.shape[1:]
+    rows, share = count * capacity, hidden // shares
+    landed = pltpu.VMEM((experts, count, capacity, both), BFLOAT)
+    flat = pltpu.VMEM((rows, hidden), BFLOAT)
+    sums = pltpu.VMEM((rows, width), SINGLE)
+    return pl.pallas_call(
+        functools.partial(expert_kernel, axis, count, shares),
+        in_specs=[ANY] * 3,
+        out_specs=[ANY] * 3,
+        out_shape=[
+            jax.ShapeDtypeStruct(x.shape, BFLOAT),
+            jax.ShapeDtypeStruct((shares, experts, width, share), BFLOAT),
+            jax.ShapeDtypeStruct((shares, experts, share, width), BFLOAT),
+        ],
+        scratch_shapes=[
+            landed,
+            landed,
+            pltpu.VMEM(w_in.shape, BFLOAT),
+            pltpu.VMEM(w_out.shape, BFLOAT),
+            flat,
+            flat,
+            sums,
+            sums,
+            pltpu.VMEM((experts, shares, width, share), BFLOAT),
+            pltpu.VMEM((experts, shares, share, width), BFLOAT),
+            pltpu.SemaphoreType.DMA((2, experts, count - 1)),
+            pltpu.SemaphoreType.DMA((2, experts, count - 1)),
+            pltpu.SemaphoreType.DMA((2, experts)),
+            pltpu.SemaphoreType.DMA((2, experts)),
+            pltpu.SemaphoreType.DMA((2, experts)),
+        ],
+        compiler_params=pltpu.CompilerParams(
+            collective_id=collective_id, has_side_effects=True, vmem_limit_bytes=58 * 2**20
+        ),
+        cost_estimate=pl.CostEstimate(
+            flops=12 * experts * rows * width * hidden,
+            bytes_accessed=8 * experts * width * hidden,
+            transcendentals=experts * rows * hidden,
+        ),
+    )(x, w_in, w_out)
 
 
 def on_device(
@@ -466,27 +541,10 @@
     send = mm(
         slot_hot, jnp.concatenate([norm_two.astype(BFLOAT), grad_routed], axis=1), TN
     ).astype(BFLOAT)
-    arrived = swap(send.reshape(n_owner, expert_dev * capacity, 2 * width), "experts", 1)
-    arrived = arrived.reshape(n_owner, expert_dev, capacity, 2 * width)
-    arrived = arrived.transpose(1, 0, 2, 3).reshape(expert_dev, n_owner * capacity, 2 * width)
-    rows, grad_expert = arrived[:, :, :width], arrived[:, :, width:]
-    pre_act = jnp.einsum("erd,edf->erf", rows, w_in, preferred_element_type=SINGLE)
-    act_bf = jax.nn.gelu(pre_act).astype(BFLOAT)
-    expert_back = jnp.einsum("erf,efd->erd", act_bf, w_out, preferred_element_type=SINGLE).astype(
-        BFLOAT
-    )
-    grad_act = jnp.einsum("erd,efd->erf", grad_expert, w_out, preferred_element_type=SINGLE)
-    grad_pre = jax.vjp(jax.nn.gelu, pre_act)[1](grad_act)[0].astype(BFLOAT)
-    grad_rows = jnp.einsum("erf,edf->erd", grad_pre, w_in, preferred_element_type=SINGLE).astype(
-        BFLOAT
-    )
-    both_back = jnp.concatenate([expert_back, grad_rows], axis=2)
-    both_back = both_back.reshape(expert_dev, n_owner, capacity, 2 * width).transpose(1, 0, 2, 3)
-    whole_in, whole_out = weight_grads(rows, grad_pre, act_bf, grad_expert, shares)
-    both_back, whole_in, whole_out = lax.optimization_barrier((both_back, whole_in, whole_out))
-    returned = swap(
-        both_back.reshape(n_owner, expert_dev * capacity, 2 * width), "experts", 2
-    ).reshape(slot_count, 2 * width)
+    returned, whole_in, whole_out = expert_layer(
+        send.reshape(n_owner, expert_dev, capacity, 2 * width), w_in, w_out, "experts", shares, 1
+    )
+    returned = returned.reshape(slot_count, 2 * width)
     grad_w_in = lax.psum_scatter(whole_in, ("context", "dp"), scatter_dimension=0, tiled=True)
     grad_w_out = lax.psum_scatter(whole_out, ("context", "dp"), scatter_dimension=0, tiled=True)
     fetched = mm(slot_hot, returned)
@@ -506,43 +564,39 @@
     grad_q, grad_pair, diagonal = attend_back(
         query_bf, pair_all, grad_attended, log_total, window, head_dim
     )
-    grad_pair = sum_shares(grad_pair.reshape(n_context, 2 * tok_count, width), "context", 3)
+    grad_query = mm(first_norm_output, grad_q, TN)
+    unit = 16 * n_owner * shares
+    grad_pair, early = reduce_all(
+        [grad_pair.reshape(2 * seq_len, width), pack([grad_query, grad_output], unit)],
+        [("context",), ("dp", "experts", "context")],
+        [False, True],
+        2,
+    )
     grad_k, grad_v = grad_pair[:tok_count], grad_pair[tok_count:]
     grad_table = jnp.einsum("ho,ob->bh", diagonal[:, 0, :], window_hot, precision=highest)
-    grad_query = mm(first_norm_output, grad_q, TN)
     grad_key = mm(first_norm_output, grad_k, TN)
     grad_value = mm(first_norm_output, grad_v, TN)
     grad_norm_one = mm(grad_q, w_query, NT) + mm(grad_k, w_key, NT) + mm(grad_v, w_value, NT)
     grad_resid, grad_gain_attn = jax.vjp(rms_scale, resid, gain_attn)[1](grad_norm_one)
     grad_tokens = grad_resid + grad_mid
-    grads = (
-        grad_query,
-        grad_key,
-        grad_value,
-        grad_output,
-        grad_gain_attn,
-        grad_gain_ffn,
-        grad_table,
-        grad_router,
-    )
-    n_all = n_owner * shares
-    small = jnp.concatenate([grad.reshape(-1) for grad in grads[4:]])
-    small_rows = -(-small.shape[0] // (128 * 8 * n_all)) * 8 * n_all
+    grads = (grad_gain_attn, grad_gain_ffn, grad_table, grad_router)
+    small = jnp.concatenate([grad.reshape(-1) for grad in grads])
+    small_rows = -(-small.shape[0] // (64 * unit)) * (unit // 2)
     small = jnp.pad(small, (0, small_rows * 128 - small.shape[0])).reshape(small_rows, 128)
-    unit = 16 * n_all
-    units = -(-4 * width // unit)
-    cut = -(-2 * units // 3) * unit
-    packed = jnp.concatenate([grad.astype(BFLOAT) for grad in grads[:4]], axis=0)
-    packed = jnp.pad(packed, ((0, units * unit - 4 * width), (0, 0)))
-    pieces, orders = [packed[:cut], small], [("dp", "context", "experts")] * 2
-    if cut < units * unit:
-        pieces.append(packed[cut:])
+    late = pack([grad_key, grad_value], unit)
+    cut = -(-2 * late.shape[0] // (3 * unit)) * unit
+    pieces, orders = [late[:cut], small], [("dp", "context", "experts")] * 2
+    if cut < late.shape[0]:
+        pieces.append(late[cut:])
         orders.append(("dp", "experts", "context"))
-    pieces = reduce_all(pieces, orders, 4)
-    packed = jnp.concatenate([pieces[0], *pieces[2:]], axis=0)
-    summed = [packed[at * width : (at + 1) * width].astype(SINGLE) for at in range(4)]
+    pieces = reduce_all(pieces, orders, [True] * len(pieces), 3)
+    late = jnp.concatenate([pieces[0], *pieces[2:]], axis=0)
+    summed = []
+    for packed in (early, late):
+        summed += [packed[:width].astype(SINGLE), packed[width : 2 * width].astype(SINGLE)]
+    summed = [summed[0], summed[2], summed[3], summed[1]]
     flat, at = pieces[1].reshape(-1), 0
-    for grad in grads[4:]:
+    for grad in grads:
         summed.append(flat[at : at + grad.size].reshape(grad.shape))
         at += grad.size
     return (

time: 395 us -> 373 us (0.944)
  matrix products: 49.1 us -> 21.7 us
  local copies, waits for them, and re-layouts: 14.3 us -> 19.8 us
  other arithmetic: 22.2 us -> 18.2 us
    pallas_call x3, Pallas kernels: 156 us -> 228 us  [the longest x2 156 us: reduce_all(): pl.pallas_call(functools.partial(reduce_kernel, orders, sizes, backs), in...]
    pallas_call x3 -> x1, Pallas kernels: 110 us -> 37.7 us  [swap(): pl.pallas_call(functools.partial(swap_kernel, axis, count, gather), in_sp...]
    dot_general x4 -> x0, matrix products: 27 us -> none  [the longest x1 7.86 us: on_device(): jnp.einsum('erd,efd->erf', grad_expert, w_out, preferred_element_type=SIN...]
    unnamed x42 -> x56, local copies, waits for them, and re-layouts: 8.63 us -> 12.4 us
  transfers between devices with their start and end apart: 2 -> 2, of which waited for: 0 -> 0; matrix products, arithmetic and copies ran while one was open for 9% -> 10% of each run, Pallas kernels for 50% -> 47%
where the time goes in v3:
time: 373 us; the launch traced here: 369 us
  Pallas kernels  294 us (79%)
  matrix products  21.7 us (6%)
  local copies, waits for them, and re-layouts  19.8 us (5%)
  other arithmetic  18.2 us (5%)
  between operations  14.5 us (4%)
    pallas_call x2, Pallas kernels, reduce_all(): pl.pallas_call(functools.partial(reduce_kernel, orders, sizes, backs), in...  156 us
    pallas_call x1, Pallas kernels, expert_layer(): pl.pallas_call(functools.partial(expert_kernel, axis, count, shares), in_...  72 us
    pallas_call x1, Pallas kernels, swap(): pl.pallas_call(functools.partial(swap_kernel, axis, count, gather), in_sp...  37.7 us
    pallas_call x1, Pallas kernels, attend_back(): pl.pallas_call(functools.partial(attend_back_kernel, head_dim), grid=(pai...  18.2 us
    dot_general x14, matrix products, mm(): return lax.dot_general(left, right, dims, preferred_element_type=SINGLE)  14.3 us
    unnamed x56, local copies, waits for them, and re-layouts  12.4 us
    pallas_call x1, Pallas kernels, attend(): pl.pallas_call(functools.partial(attend_kernel, head_dim), grid=(pairs,),...  9.88 us
  transfers between devices with their start and end apart: 2, of which 0 were waited for; matrix products, arithmetic and copies ran while one was open for 10% of the time, Pallas kernels for 47%

profile of v3, /device:TPU:25, one launch (start us, length us, event | category | flops | bytes accessed | tf_op | source)
XLA Modules:
  0.0 369.1 jit_solution(11616671422677600249)
XLA Ops:
  7.3 1.3 fusion.9
  8.6 0.9 pad_dynamic-slice_fusion
  9.4 1.2 convolution_bitcast_fusion
  10.7 1.9 convolution_convert_fusion.8.q_ref
  12.7 0.5 convolution_convert_fusion.7
  13.2 0.5 convolution_convert_fusion.6
  13.8 0.9 pad_maximum_fusion.3.x_ref
  14.7 37.7 %shard_map.238 = bf16[4,256,1536]{2,1,0:T(8,128)(2,1)} custom-call(bf16[256,1536]{1,0:T(8,128)(2,1)} %pad_maximum_fusion.3.x_ref), custom_call_target="tpu_custom_call" | custom-call | tf_op jit(solution)/shard_map/pallas_call | solution.py:219
  52.4 1.9 copy-done.1
  54.2 9.9 %shard_map.239 = (bf16[256,768]{1,0:T(8,128)(2,1)S(1)}, f32[12,256,1]{2,1,0:T(8,128)S(1)}) custom-call(bf16[256,768]{1,0:T(8,128)(2,1)S(1)} %convolution_convert_fusion.8.q_ref, bf16[1024,1536]{1,0:T(8,128)(2,1)S(1)} %bitcast.64, bf16[1024,1536]{1,0:T(8,128)(2,1)S(1)} %bitcast.65, f32[12,1,1280]{2,1,0:T(1,128)S(1)} %broadcast_in_dim.11.win_ref), custom_call_target="tpu_custom_call" | custom-call | flops 805306368 | bytes 3932160 | tf_op jit(solution)/shard_map/pallas_call | solution.py:108
  64.2 0.6 multiply_reduce_fusion.2
  65.1 0.8 fusion.61
  66.2 1.8 convolution_convert_fusion
  68.0 72.0 %shard_map.240 = (bf16[4,2,64,1536]{3,2,1,0:T(8,128)(2,1)}, bf16[8,2,768,384]{3,2,1,0:T(8,128)(2,1)}, bf16[8,2,384,768]{3,2,1,0:T(8,128)(2,1)}) custom-call(bf16[4,2,64,1536]{3,2,1,0:T(8,128)(2,1)} %bitcast.73, bf16[2,768,3072]{2,1,0:T(8,128)(2,1)} %win_ref.1, bf16[2,3072,768]{2,1,0:T(8,128)(2,1)} %wout_ref.1), custom_call_target="tpu_custom_call" | custom-call | flops 14495514624 | bytes 37748736 | tf_op jit(solution)/shard_map/pallas_call | solution.py:439
  140.3 0.5 reduce-scatter.3.cloned.1.call-update
  140.8 2.1 fusion.18
  142.9 1.1 copy-done.12
  144.1 1.0 fusion.8
  145.0 2.2 fusion.15
  147.2 1.2 reshape.178
  148.4 2.5 multiply_reduce_fusion
  151.2 1.3 copy-done.14
  153.3 1.1 copy-done.7
  154.4 18.2 %shard_map.241 = (bf16[256,768]{1,0:T(8,128)(2,1)S(1)}, bf16[4,2,256,768]{3,2,1,0:T(8,128)(2,1)S(1)}, f32[12,1,1280]{2,1,0:T(1,128)S(1)}) custom-call(bf16[256,768]{1,0:T(8,128)(2,1)S(1)} %convolution_convert_fusion.8.q_ref, bf16[1024,1536]{1,0:T(8,128)(2,1)} %bitcast.62, bf16[1024,1536]{1,0:T(8,128)(2,1)} %bitcast.63, ...), custom_call_target="tpu_custom_call" | custom-call | flops 2415919104 | bytes 7864320 | tf_op jit(solution)/shard_map/pallas_call | solution.py:133
  172.6 1.7 copy-done.2
  174.2 0.7 fusion.28
  175.1 1.6 convolution_convert_fusion.4
  177.4 113.5 %shard_map.242 = (bf16[512,768]{1,0:T(8,128)(2,1)S(1)}, bf16[1536,768]{1,0:T(8,128)(2,1)S(1)}) custom-call(bf16[2048,768]{1,0:T(8,128)(2,1)} %bitcast.66, bf16[1536,768]{1,0:T(8,128)(2,1)S(1)} %pad_maximum_fusion.refs_1_), custom_call_target="tpu_custom_call" | custom-call | tf_op jit(solution)/shard_map/pallas_call | solution.py:319
  291.0 0.6 convolution_convert_fusion.1
  291.6 0.7 copy-done.3
  292.3 0.7 copy-done.19
  293.6 0.8 copy-done.18
  294.9 2.0 fusion.4
  296.9 0.6 convolution_convert_fusion.2
  297.6 42.9 %shard_map.243 = (bf16[1024,768]{1,0:T(8,128)(2,1)S(1)}, f32[256,128]{1,0:T(8,128)S(1)}, bf16[512,768]{1,0:T(8,128)(2,1)S(1)}) custom-call(bf16[1024,768]{1,0:T(8,128)(2,1)S(1)} %pad_maximum_fusion.1.refs_0_, f32[256,128]{1,0:T(8,128)S(1)} %fusion.36.refs_1_, bf16[512,768]{1,0:T(8,128)(2,1)S(1)} %slice.69.refs_2_), custom_call_target="tpu_custom_call" | custom-call | tf_op jit(solution)/shard_map/pallas_call | solution.py:319
  340.5 0.6 slice.65
  341.2 0.6 slice.66
  341.8 0.8 reshape.180
  342.6 0.7 copy.31
  343.2 1.7 reshape.181
  344.9 1.7 copy.32
  346.7 0.9 multiply_multiply_fusion.3
  347.5 1.4 slice_bitcast_fusion
  348.9 2.6 fusion.6
  351.5 2.5 slice_convert_fusion
  354.1 2.5 fusion
  356.6 2.8 bitcast_convert_fusion
  359.5 2.8 bitcast_convert_fusion.1
  (69 shorter events, 4.1 us)
Async XLA Ops:
  7.2 6.0 %copy-start = (bf16[768,768]{1,0:T(8,128)(2,1)S(1)}, bf16[768,768]{1,0:T(8,128)(2,1)}, u32[]{:S(2)}) copy-start(bf16[768,768]{1,0:T(8,128)(2,1)} %param.19) | copy-start | bytes 3538948
  7.2 5.5 %copy-start.10 = (bf16[1,256,768]{2,1,0:T(8,128)(2,1)S(1)}, bf16[1,256,768]{2,1,0:T(8,128)(2,1)}, u32[]{:S(2)}) copy-start(bf16[1,256,768]{2,1,0:T(8,128)(2,1)} %param.15) | copy-start | bytes 1179652
  7.2 5.5 %copy-start.22 = (f32[768]{0:T(1024)S(1)}, f32[768]{0:T(1024)}, u32[]{:S(2)}) copy-start(f32[768]{0:T(1024)} %param.21) | copy-start | bytes 9220
  7.2 349.4 %reduce-scatter.5.cloned.1.call-start = ((), (), s32[]{:S(2)}) async-start(), calls=%async_computation.3 | async-start | bytes 10616832 | tf_op jit(solution)/shard_map/reduce_scatter | solution.py:549
  8.5 4.7 %copy-start.25 = (f32[256]{0:T(256)}, f32[256]{0:T(256)S(1)}, u32[]{:S(2)}) copy-start(f32[256]{0:T(256)S(1)} %fusion.9) | copy-start | bytes 3076
  8.5 288.3 %copy-start.23 = (f32[256]{0:T(256)}, f32[256]{0:T(256)S(1)}, u32[]{:S(2)}) copy-start(f32[256]{0:T(256)S(1)} %fusion.50) | copy-start | bytes 3076
  8.6 4.1 %copy-start.17 = (bf16[768,768]{1,0:T(8,128)(2,1)S(1)}, bf16[768,768]{1,0:T(8,128)(2,1)}, u32[]{:S(2)}) copy-start(bf16[768,768]{1,0:T(8,128)(2,1)} %param.18) | copy-start | bytes 3538948
  52.4 1.9 copy-start.1
  54.2 10.0 %copy-start.13 = (bf16[768,768]{1,0:T(8,128)(2,1)S(1)}, bf16[768,768]{1,0:T(8,128)(2,1)}, u32[]{:S(2)}) copy-start(bf16[768,768]{1,0:T(8,128)(2,1)} %param.20) | copy-start | bytes 3538948
  64.1 1.8 copy-start.6
  64.1 0.7 copy-start.24
  64.2 0.8 copy-start.26
  64.2 0.8 copy-start.20
  64.2 0.9 copy-start.21
  64.2 1.8 copy-start.15
  140.1 219.4 %reduce-scatter.3.cloned.1.call-start = ((), (), s32[]{:S(2)}) async-start(), calls=%async_computation.2 | async-start | bytes 10616832 | tf_op jit(solution)/shard_map/reduce_scatter | solution.py:548
  140.8 3.2 copy-start.16
  142.9 1.1 copy-start.12
  150.9 1.5 copy-start.14
  152.4 0.9 copy-start.8
  152.4 2.0 copy-start.7
  172.6 1.7 copy-start.2
  174.2 2.4 copy-start.9
  177.4 113.6 %copy-start.11 = (bf16[1,256,768]{2,1,0:T(8,128)(2,1)S(1)}, bf16[1,256,768]{2,1,0:T(8,128)(2,1)}, u32[]{:S(2)}) copy-start(bf16[1,256,768]{2,1,0:T(8,128)(2,1)} %param.15) | copy-start | bytes 1179652
  290.9 1.4 copy-start.3
  290.9 2.1 copy-start.19
  293.1 1.3 copy-start.18
  340.5 0.7 copy-start.5
  346.7 4.8 %copy-start.4 = (bf16[1536,768]{1,0:T(8,128)(2,1)S(1)}, bf16[1536,768]{1,0:T(8,128)(2,1)}, u32[]{:S(2)}) copy-start(bf16[1536,768]{1,0:T(8,128)(2,1)} %copy-done.3) | copy-start | bytes 7077892
Sparse Core Ops, SparseCore 0:
  140.2 103.9 reduce-scatter.4
  247.6 84.2 reduce-scatter.2

commit v4 on v3

--- a/solution.py
+++ b/solution.py
@@ -345,16 +345,18 @@
 
 
 def expert_kernel(
-    axis, count, shares, x_ref, win_ref, wout_ref, back_ref, gin_ref, gout_ref,
-    arrived, leaving, w_in, w_out, act, grad_pre, total, grad_total, whole_in, whole_out,
-    send_sem, recv_sem, own_sem, load_sem, store_sem,
+    axis, count, shares, x_ref, win_ref, wout_ref, back_ref, own_ref, held_ref,
+    arrived, leaving, w_in, w_out, act, grad_pre, total, grad_total, whole,
+    send_sem, recv_sem, own_sem, load_sem, store_sem, half_sem,
 ):
     experts, _, capacity, both = arrived.shape
     width, hidden, rows = both // 2, w_in.shape[2], count * capacity
     share = hidden // shares
     me = lax.axis_index(axis)
     peers = [lax.rem(me + step, count) for step in range(1, count)]
-    greet([{axis: peer} for peer in peers])
+    mine = lax.axis_index("dp")
+    other = 1 - mine
+    greet([{axis: peer} for peer in peers] + [{"dp": other}])
     loads, coming = [], []
     for e in range(experts):
         here = [
@@ -413,18 +415,21 @@
 
         def weigh(at, carry):
             cut = pl.ds(pl.multiple_of(at * share, share), share)
-            whole_in[e, at] = mm(came, grad_pre[:, cut], TN).astype(BFLOAT)
-            whole_out[e, at] = mm(act[:, cut], grad, TN).astype(BFLOAT)
+            half, place = lax.rem(at, 2), at // 2
+            whole[e, half, place, 0] = mm(came, grad_pre[:, cut], TN).astype(BFLOAT)
+            whole[e, half, place, 1] = mm(grad, act[:, cut], TN).astype(BFLOAT)
             return carry
 
         lax.fori_loop(0, shares, weigh, 0)
-        pair = [
-            pltpu.make_async_copy(whole_in.at[e], gin_ref.at[:, e], store_sem.at[0, e]),
-            pltpu.make_async_copy(whole_out.at[e], gout_ref.at[:, e], store_sem.at[1, e]),
-        ]
-        for copy in pair:
-            copy.start()
-        stores += pair
+        stores.append(
+            remote(
+                whole.at[e, other], held_ref.at[e],
+                half_sem.at[0, e], half_sem.at[1, e], {"dp": other},
+            )
+        )
+        own = pltpu.make_async_copy(whole.at[e, mine], own_ref.at[e], store_sem.at[e])
+        own.start()
+        stores.append(own)
     for copy in leave + stores:
         copy.wait()
 
@@ -442,8 +447,8 @@
         out_specs=[ANY] * 3,
         out_shape=[
             jax.ShapeDtypeStruct(x.shape, BFLOAT),
-            jax.ShapeDtypeStruct((shares, experts, width, share), BFLOAT),
-            jax.ShapeDtypeStruct((shares, experts, share, width), BFLOAT),
+            jax.ShapeDtypeStruct((experts, shares // 2, 2, width, share), BFLOAT),
+            jax.ShapeDtypeStruct((experts, shares // 2, 2, width, share), BFLOAT),
         ],
         scratch_shapes=[
             landed,
@@ -454,12 +459,12 @@
             flat,
             sums,
             sums,
-            pltpu.VMEM((experts, shares, width, share), BFLOAT),
-            pltpu.VMEM((experts, shares, share, width), BFLOAT),
+            pltpu.VMEM((experts, 2, shares // 2, 2, width, share), BFLOAT),
             pltpu.SemaphoreType.DMA((2, experts, count - 1)),
             pltpu.SemaphoreType.DMA((2, experts, count - 1)),
             pltpu.SemaphoreType.DMA((2, experts)),
             pltpu.SemaphoreType.DMA((2, experts)),
+            pltpu.SemaphoreType.DMA((experts,)),
             pltpu.SemaphoreType.DMA((2, experts)),
         ],
         compiler_params=pltpu.CompilerParams(
@@ -541,12 +546,24 @@
     send = mm(
         slot_hot, jnp.concatenate([norm_two.astype(BFLOAT), grad_routed], axis=1), TN
     ).astype(BFLOAT)
-    returned, whole_in, whole_out = expert_layer(
+    returned, own_half, held_half = expert_layer(
         send.reshape(n_owner, expert_dev, capacity, 2 * width), w_in, w_out, "experts", shares, 1
     )
     returned = returned.reshape(slot_count, 2 * width)
-    grad_w_in = lax.psum_scatter(whole_in, ("context", "dp"), scatter_dimension=0, tiled=True)
-    grad_w_out = lax.psum_scatter(whole_out, ("context", "dp"), scatter_dimension=0, tiled=True)
+    context = lax.axis_index("context")
+
+    def half_sum(at):
+        own = lax.dynamic_index_in_dim(own_half, at, 1, keepdims=False).astype(SINGLE)
+        return own + lax.dynamic_index_in_dim(held_half, at, 1, keepdims=False).astype(SINGLE)
+
+    expert_shares = [
+        lax.ppermute(
+            half_sum(context ^ step).astype(BFLOAT),
+            "context",
+            [(at, at ^ step) for at in range(n_context)],
+        )
+        for step in range(1, n_context)
+    ]
     fetched = mm(slot_hot, returned)
     routed = fetched[:, :width]
     output = residual_middle + gate[:, None] * routed
@@ -599,6 +616,9 @@
     for grad in grads:
         summed.append(flat[at : at + grad.size].reshape(grad.shape))
         at += grad.size
+    expert_sum = half_sum(context)
+    for arrived in expert_shares:
+        expert_sum = expert_sum + arrived.astype(SINGLE)
     return (
         output.astype(BFLOAT)[None],
         grad_tokens[None],
@@ -610,8 +630,8 @@
         summed[5],
         summed[6],
         summed[7],
-        grad_w_in[0].astype(SINGLE),
-        grad_w_out[0].astype(SINGLE),
+        expert_sum[:, 0],
+        expert_sum[:, 1].transpose(0, 2, 1),
     )
 
 

time: 373 us -> 414 us (1.11)
  Pallas kernels: 294 us -> 339 us
  between operations: 14.5 us -> 1.16 us
  other arithmetic: 18.2 us -> 29.3 us
    pallas_call x2, Pallas kernels: 156 us -> 202 us  [reduce_all(): pl.pallas_call(functools.partial(reduce_kernel, orders, sizes, backs), in...]
    add x0 -> x1, other arithmetic: none -> 5.82 us  [on_device(): expert_sum = expert_sum + arrived.astype(SINGLE)]
    convert_element_type x2, other arithmetic: 5.67 us -> 10.2 us  [on_device(): half_sum(context ^ step).astype(BFLOAT)]
    unnamed x56 -> x57, local copies, waits for them, and re-layouts: 12.4 us -> 10.4 us
  transfers between devices with their start and end apart: 2 -> 3, of which waited for: 0 -> 0; matrix products, arithmetic and copies ran while one was open for 10% -> 9% of each run, Pallas kernels for 47% -> 53%
where the time goes in v4:
time: 414 us; the launch traced here: 413 us
  Pallas kernels  339 us (82%)
  other arithmetic  29.3 us (7%)
  local copies, waits for them, and re-layouts  20.7 us (5%)
  matrix products  19.7 us (5%)
    pallas_call x2, Pallas kernels, reduce_all(): pl.pallas_call(functools.partial(reduce_kernel, orders, sizes, backs), in...  202 us
    pallas_call x1, Pallas kernels, expert_layer(): pl.pallas_call(functools.partial(expert_kernel, axis, count, shares), in_...  71.3 us
    pallas_call x1, Pallas kernels, swap(): pl.pallas_call(functools.partial(swap_kernel, axis, count, gather), in_sp...  37.7 us
    pallas_call x1, Pallas kernels, attend_back(): pl.pallas_call(functools.partial(attend_back_kernel, head_dim), grid=(pai...  18.1 us
    dot_general x14, matrix products, mm(): return lax.dot_general(left, right, dims, preferred_element_type=SINGLE)  13.6 us
    unnamed x57, local copies, waits for them, and re-layouts  10.4 us
    convert_element_type x2, other arithmetic, on_device(): half_sum(context ^ step).astype(BFLOAT)  10.2 us
    pallas_call x1, Pallas kernels, attend(): pl.pallas_call(functools.partial(attend_kernel, head_dim), grid=(pairs,),...  9.88 us
  transfers between devices with their start and end apart: 3, of which 0 were waited for; matrix products, arithmetic and copies ran while one was open for 9% of the time, Pallas kernels for 53%

profile of v4, /device:TPU:25, one launch (start us, length us, event | category | flops | bytes accessed | tf_op | source)
XLA Modules:
  0.0 412.9 jit_solution(5373991239834064494)
XLA Ops:
  0.7 0.9 pad_dynamic-slice_fusion
  1.6 1.2 convolution_bitcast_fusion
  2.9 1.2 fusion.14
  4.1 1.5 convolution_convert_fusion.6
  6.2 0.9 pad_maximum_fusion.3.x_ref
  7.1 37.7 %shard_map.238 = bf16[4,256,1536]{2,1,0:T(8,128)(2,1)} custom-call(bf16[256,1536]{1,0:T(8,128)(2,1)} %pad_maximum_fusion.3.x_ref), custom_call_target="tpu_custom_call" | custom-call | tf_op jit(solution)/shard_map/pallas_call | solution.py:219
  45.4 1.9 copy-done.1
  47.2 9.9 %shard_map.239 = (bf16[256,768]{1,0:T(8,128)(2,1)S(1)}, f32[12,256,1]{2,1,0:T(8,128)S(1)}) custom-call(bf16[256,768]{1,0:T(8,128)(2,1)S(1)} %convolution_convert_fusion.8.q_ref, bf16[1024,1536]{1,0:T(8,128)(2,1)S(1)} %bitcast.76, bf16[1024,1536]{1,0:T(8,128)(2,1)S(1)} %bitcast.77, f32[12,1,1280]{2,1,0:T(1,128)S(1)} %broadcast_in_dim.11.win_ref), custom_call_target="tpu_custom_call" | custom-call | flops 805306368 | bytes 3932160 | tf_op jit(solution)/shard_map/pallas_call | solution.py:108
  57.1 1.1 copy-done.6
  58.3 0.6 multiply_reduce_fusion.2
  59.0 0.8 fusion.66
  60.0 1.0 fusion.12
  61.0 2.9 convolution_convert_fusion
  64.0 71.3 %shard_map.240 = (bf16[4,2,64,1536]{3,2,1,0:T(8,128)(2,1)}, bf16[2,4,2,768,384]{4,3,2,1,0:T(8,128)(2,1)}, bf16[2,4,2,768,384]{4,3,2,1,0:T(8,128)(2,1)}) custom-call(bf16[4,2,64,1536]{3,2,1,0:T(8,128)(2,1)} %bitcast.85, bf16[2,768,3072]{2,1,0:T(8,128)(2,1)} %win_ref.1, bf16[2,3072,768]{2,1,0:T(8,128)(2,1)} %wout_ref.1), custom_call_target="tpu_custom_call" | custom-call | flops 14495514624 | bytes 37748736 | tf_op jit(solution)/shard_map/pallas_call | solution.py:444
  135.3 5.7 %fusion.2 = (bf16[2,2,768,384]{3,2,1,0:T(8,128)(2,1)}, bf16[2,2,768,384]{3,2,1,0:T(8,128)(2,1)}) fusion(s32[]{:T(128)S(6)} %select_n.53, s32[]{:T(128)S(6)} %select_n.54, bf16[2,4,2,768,384]{4,3,2,1,0:T(8,128)(2,1)} %get-tuple-element.36, bf16[2,4,2,768,384]{4,3,2,1,0:T(8,128)(2,1)} %get-tuple-element.37), kind=kLoop, calls=%fused_computation.7 | loop fusion | flops 9437184 | bytes 14155784 | tf_op jit(solution)/shard_map/convert_element_type | solution.py:561
  141.0 1.6 collective-permute-start.1
  142.7 4.5 %fusion.4 = bf16[2,2,768,384]{3,2,1,0:T(8,128)(2,1)} fusion(bf16[2,4,2,768,384]{4,3,2,1,0:T(8,128)(2,1)} %get-tuple-element.37, s32[]{:T(128)S(6)} %select_n.55, bf16[2,4,2,768,384]{4,3,2,1,0:T(8,128)(2,1)} %get-tuple-element.36), kind=kLoop, calls=%fused_computation.9 | loop fusion | flops 4718592 | bytes 7077892 | tf_op jit(solution)/shard_map/convert_element_type | solution.py:561
  147.1 1.1 collective-permute-start.2
  148.3 0.6 fusion.23
  148.9 1.0 fusion.13
  149.9 2.2 fusion.20
  152.1 1.1 multiply_reduce_fusion
  154.0 0.7 copy-done.11
  155.3 18.1 %shard_map.241 = (bf16[256,768]{1,0:T(8,128)(2,1)S(1)}, bf16[4,2,256,768]{3,2,1,0:T(8,128)(2,1)S(1)}, f32[12,1,1280]{2,1,0:T(1,128)S(1)}) custom-call(bf16[256,768]{1,0:T(8,128)(2,1)S(1)} %convolution_convert_fusion.8.q_ref, bf16[1024,1536]{1,0:T(8,128)(2,1)} %bitcast.74, bf16[1024,1536]{1,0:T(8,128)(2,1)} %bitcast.75, ...), custom_call_target="tpu_custom_call" | custom-call | flops 2415919104 | bytes 7864320 | tf_op jit(solution)/shard_map/pallas_call | solution.py:133
  173.4 0.6 convolution_convert_fusion.4
  174.0 1.5 copy-done.19
  176.2 161.5 %shard_map.242 = (bf16[512,768]{1,0:T(8,128)(2,1)S(1)}, bf16[1536,768]{1,0:T(8,128)(2,1)S(1)}) custom-call(bf16[2048,768]{1,0:T(8,128)(2,1)} %bitcast.78, bf16[1536,768]{1,0:T(8,128)(2,1)S(1)} %pad_maximum_fusion.refs_1_), custom_call_target="tpu_custom_call" | custom-call | tf_op jit(solution)/shard_map/pallas_call | solution.py:319
  337.7 1.6 convolution_convert_fusion.1
  340.4 0.7 fusion.33
  341.1 1.2 reshape.189
  342.4 1.2 slice.77.refs_2_
  343.6 2.0 fusion.9
  345.7 0.6 convolution_convert_fusion.2
  346.4 40.9 %shard_map.243 = (bf16[1024,768]{1,0:T(8,128)(2,1)S(1)}, f32[256,128]{1,0:T(8,128)S(1)}, bf16[512,768]{1,0:T(8,128)(2,1)S(1)}) custom-call(bf16[1024,768]{1,0:T(8,128)(2,1)S(1)} %pad_maximum_fusion.1.refs_0_, f32[256,128]{1,0:T(8,128)S(1)} %fusion.41.refs_1_, bf16[512,768]{1,0:T(8,128)(2,1)S(1)} %slice.77.refs_2_), custom_call_target="tpu_custom_call" | custom-call | tf_op jit(solution)/shard_map/pallas_call | solution.py:319
  387.3 0.6 slice.72
  388.0 0.6 slice.71
  388.6 1.7 reshape.192
  390.3 1.7 copy.45
  392.0 0.8 reshape.191
  392.8 0.7 copy.44
  393.5 0.9 multiply_multiply_fusion.3
  394.3 1.4 slice_bitcast_fusion.2
  395.7 2.6 fusion.11
  398.3 2.5 slice_convert_fusion
  400.9 2.5 fusion.5
  403.4 5.8 %fusion.1 = f32[2,2,768,384]{3,2,1,0:T(8,128)S(1)} fusion(bf16[2,2,768,384]{3,2,1,0:T(8,128)(2,1)} %collective-permute-done.2, bf16[2,2,768,384]{3,2,1,0:T(8,128)(2,1)} %collective-permute-done.1, bf16[2,2,768,384]{3,2,1,0:T(8,128)(2,1)} %collective-permute-done, s32[]{:T(128)S(6)} %select_n.52, bf16[2,4,2,768,384]{4,3,2,1,0:T(8,128)(2,1)} %get-tuple-element.36, ...), kind=kLoop, calls=%fused_computation.2 | loop fusion | flops 10616832 | bytes 16515076 | tf_op jit(solution)/shard_map/add | solution.py:621
  409.2 1.7 slice_bitcast_fusion
  411.0 1.9 copy.46
  (72 shorter events, 4.7 us)
Async XLA Ops:
  0.6 3.4 copy-start
  0.7 5.0 %copy-start.9 = (bf16[1,256,768]{2,1,0:T(8,128)(2,1)S(1)}, bf16[1,256,768]{2,1,0:T(8,128)(2,1)}, u32[]{:S(2)}) copy-start(bf16[1,256,768]{2,1,0:T(8,128)(2,1)} %param.15) | copy-start | bytes 1179652
  0.7 5.0 %copy-start.22 = (f32[768]{0:T(1024)S(1)}, f32[768]{0:T(1024)}, u32[]{:S(2)}) copy-start(f32[768]{0:T(1024)} %param.21) | copy-start | bytes 9220
  0.7 5.0 %copy-start.16 = (bf16[768,768]{1,0:T(8,128)(2,1)S(1)}, bf16[768,768]{1,0:T(8,128)(2,1)}, u32[]{:S(2)}) copy-start(bf16[768,768]{1,0:T(8,128)(2,1)} %param.18) | copy-start | bytes 3538948
  4.1 3.1 copy-start.25
  4.1 341.6 %copy-start.23 = (f32[256]{0:T(256)}, f32[256]{0:T(256)S(1)}, u32[]{:S(2)}) copy-start(f32[256]{0:T(256)S(1)} %fusion.55) | copy-start | bytes 3076
  6.2 38.6 %copy-start.18 = (bf16[768,768]{1,0:T(8,128)(2,1)S(1)}, bf16[768,768]{1,0:T(8,128)(2,1)}, u32[]{:S(2)}) copy-start(bf16[768,768]{1,0:T(8,128)(2,1)} %param.17) | copy-start | bytes 3538948
  45.3 1.9 copy-start.1
  47.2 11.1 %copy-start.10 = (bf16[768,768]{1,0:T(8,128)(2,1)S(1)}, bf16[768,768]{1,0:T(8,128)(2,1)}, u32[]{:S(2)}) copy-start(bf16[768,768]{1,0:T(8,128)(2,1)} %param.20) | copy-start | bytes 3538948
  57.1 1.1 copy-start.6
  58.3 0.7 copy-start.20
  58.3 0.8 copy-start.21
  58.3 1.6 copy-start.24
  58.3 1.7 copy-start.26
  58.3 1.7 copy-start.12
  141.0 262.4 %collective-permute-start = (bf16[2,2,768,384]{3,2,1,0:T(8,128)(2,1)}, bf16[2,2,768,384]{3,2,1,0:T(8,128)(2,1)}, u32[]{:S(2)}, u32[]{:S(2)}) collective-permute-start(bf16[2,2,768,384]{3,2,1,0:T(8,128)(2,1)} %get-tuple-element.66), channel_id=1, source_target_pairs={{0,2},{2,0},{4,6},{6,4},{1,3},{3,1},{5,7},{7,5},{8,10},{10,8},{12,... | collective-permute-start | bytes 7077896 | tf_op jit(solution)/shard_map/ppermute | solution.py:560
  141.0 262.4 %collective-permute-start.1 = (bf16[2,2,768,384]{3,2,1,0:T(8,128)(2,1)}, bf16[2,2,768,384]{3,2,1,0:T(8,128)(2,1)}, u32[]{:S(2)}, u32[]{:S(2)}) collective-permute-start(bf16[2,2,768,384]{3,2,1,0:T(8,128)(2,1)} %get-tuple-element.67), channel_id=1, source_target_pairs={{0,4},{2,6},{4,0},{6,2},{1,5},{3,7},{5,1},{7,3},{8,12},{10,14},{12... | collective-permute-start | bytes 7077896 | tf_op jit(solution)/shard_map/ppermute | solution.py:560
  142.7 5.6 %copy-start.15 = (bf16[4,2,64,1536]{3,2,1,0:T(8,128)(2,1)S(1)}, bf16[4,2,64,1536]{3,2,1,0:T(8,128)(2,1)}, u32[]{:S(2)}) copy-start(bf16[4,2,64,1536]{3,2,1,0:T(8,128)(2,1)} %get-tuple-element.26) | copy-start | bytes 4718596
  147.1 1.8 copy-start.13
  147.1 256.3 %collective-permute-start.2 = (bf16[2,2,768,384]{3,2,1,0:T(8,128)(2,1)}, bf16[2,2,768,384]{3,2,1,0:T(8,128)(2,1)}, u32[]{:S(2)}, u32[]{:S(2)}) collective-permute-start(bf16[2,2,768,384]{3,2,1,0:T(8,128)(2,1)} %fusion.4), channel_id=1, source_target_pairs={{0,6},{2,4},{4,2},{6,0},{1,7},{3,5},{5,3},{7,1},{8,14},{10,12},{12... | collective-permute-start | bytes 7077896 | tf_op jit(solution)/shard_map/ppermute | solution.py:560
  153.2 1.5 copy-start.11
  153.4 1.7 copy-start.8
  153.5 1.8 copy-start.7
  173.4 2.8 copy-start.2
  173.4 2.1 copy-start.19
  337.7 2.7 copy-start.3
  337.7 2.1 copy-start.17
  343.6 2.7 copy-start.14
  387.3 0.7 copy-start.5
  393.5 4.8 %copy-start.4 = (bf16[1536,768]{1,0:T(8,128)(2,1)S(1)}, bf16[1536,768]{1,0:T(8,128)(2,1)}, u32[]{:S(2)}) copy-start(bf16[1536,768]{1,0:T(8,128)(2,1)} %copy-done.3) | copy-start | bytes 7077892
